TPU v7x, 256 devices: a whole 4x4x8 slice. The times are simulated.
256 devices in a mesh: cache: 16 (over x, y), tensor: 16 (over z, core).
Axes of the slice: x: 4, y: 4, z: 8, core: 2. Of those that a mesh axis runs over, the one named last changes fastest.
Arguments:
- hidden: bfloat16 [128, 128, 2048], P('cache'), may hold values from -6 to 6
- lengths: int32 [128], replicated, may hold values from 1 to 128, 10240 in all
- owners: int32 [128], replicated, may hold values from 0 to 15, as said below
- slot_ids: int32 [128], replicated, may hold values from 0 to 15, as said below
- state_cache: float32 [256, 32, 128, 128], P('cache', 'tensor'), may hold values from -6 to 6
- conv_cache: bfloat16 [256, 3, 16, 512], P('cache', None, 'tensor'), may hold values from -6 to 6
- w_qkvz: bfloat16 [2048, 16, 768], P(None, 'tensor'), may hold values from -0.125 to 0.125
- w_beta_alpha: bfloat16 [2048, 16, 4], P(None, 'tensor'), may hold values from -0.125 to 0.125
- conv_weight: bfloat16 [4, 16, 512], P(None, 'tensor'), may hold values from -3 to 3
- decay_log: float32 [32], P('tensor'), may hold values from -1 to 2
- step_bias: float32 [32], P('tensor'), may hold values from -6 to -4
- norm_gain: float32 [128], replicated, may hold values from 0.1 to 1.9
- w_out: bfloat16 [4096, 2048], P('tensor'), may hold values from -0.125 to 0.125
Outputs:
- layer_out: bfloat16 [128, 128, 2048], P('cache', None, 'tensor')
- new_state_cache: float32 [256, 32, 128, 128], P('cache', 'tensor')
- new_conv_cache: bfloat16 [256, 3, 16, 512], P('cache', None, 'tensor')
Inputs may be any that keep to these rules, and one draw needn't show every extreme that they name: `owners`: no two conversations share an owner and a slot. At most 16 conversations have one owner, and one owner has exactly that many; among the 8 conversations of one index of the cache axis at most 1 have one owner, and some have exactly that many. Every owner holds at least one conversation. `slot_ids`: slots of one owner's conversations are distinct.
All inputs are finite; a program needn't handle non-finite values.
Results may differ from a plain program's by a relative error of at most 0.009.
Values may be sent and summed in bfloat16 or wider, within the bound.
A program may use at most 128 MiB of HBM per device.

v0:
```python
import math

import jax
import jax.numpy as jnp
from jax import lax
from jax.sharding import PartitionSpec as P

BLOCK = 64


HIGHEST_PREC = lax.Precision.HIGHEST


def unit_lower_inverse(lower_part):
    span = lower_part.shape[-1]
    identity_mat = jnp.eye(span, dtype=lower_part.dtype)
    power = -lower_part
    inverse = identity_mat + power
    for level in range((span - 1).bit_length() - 1):
        power = jnp.einsum("...ij,...jk->...ik", power, power, precision=HIGHEST_PREC)
        inverse = inverse + jnp.einsum("...ij,...jk->...ik", inverse, power, precision=HIGHEST_PREC)
    return inverse


def block_step(memory, block_in):
    queries, key_rows, values, decays, beta_gate = block_in
    span = decays.shape[-1]
    cumulative = jnp.cumsum(decays, axis=-1)
    row_ids = lax.broadcasted_iota(jnp.int32, (span, span), 0)
    col_ids = lax.broadcasted_iota(jnp.int32, (span, span), 1)
    inclusive = row_ids >= col_ids
    strictly = row_ids > col_ids
    log_gaps = cumulative[..., :, None] - cumulative[..., None, :]
    weighting = jnp.where(inclusive, jnp.exp(jnp.where(inclusive, log_gaps, 0.0)), 0.0)
    key_intersection = jnp.einsum("...id,...jd->...ij", key_rows, key_rows, precision=HIGHEST_PREC)
    lower_part = jnp.where(strictly, beta_gate[..., :, None] * key_intersection * weighting, 0.0)
    growth = jnp.exp(cumulative)
    right_side = jnp.concatenate(
        [(beta_gate * growth)[..., None] * key_rows, beta_gate[..., None] * values], axis=-1
    )
    inverse = unit_lower_inverse(lower_part)
    solved = jnp.einsum("...ij,...jk->...ik", inverse, right_side, precision=HIGHEST_PREC)
    key_dim = key_rows.shape[-1]
    updates = solved[..., key_dim:] - jnp.einsum(
        "...ld,...de->...le", solved[..., :key_dim], memory, precision=HIGHEST_PREC
    )
    scores = jnp.einsum("...id,...jd->...ij", queries, key_rows, precision=HIGHEST_PREC) * weighting
    outputs = jnp.einsum(
        "...ld,...de->...le", queries * growth[..., None], memory, precision=HIGHEST_PREC
    )
    outputs = outputs + jnp.einsum("...ij,...je->...ie", scores, updates, precision=HIGHEST_PREC)
    final_log = cumulative[..., -1:]
    fading = jnp.exp(final_log - cumulative)
    memory = jnp.exp(final_log)[..., None] * memory + jnp.einsum(
        "...ld,...le->...de", key_rows * fading[..., None], updates, precision=HIGHEST_PREC
    )
    return (memory, outputs)


def delta_rule(memory, queries, key_rows, values, decays, beta_gate):
    positions = decays.shape[-1]
    block_count = positions // BLOCK

    def to_blocks(array_in):
        shaped = array_in.reshape(array_in.shape[:-2] + (block_count, BLOCK, array_in.shape[-1]))
        return jnp.moveaxis(shaped, -3, 0)

    def to_blocks_flat(array_in):
        shaped = array_in.reshape(array_in.shape[:-1] + (block_count, BLOCK))
        return jnp.moveaxis(shaped, -2, 0)

    final_memory, outputs = lax.scan(
        block_step,
        memory,
        (
            to_blocks(queries),
            to_blocks(key_rows),
            to_blocks(values),
            to_blocks_flat(decays),
            to_blocks_flat(beta_gate),
        ),
    )
    outputs = jnp.moveaxis(outputs, 0, -3)
    outputs = outputs.reshape(outputs.shape[:-3] + (positions, outputs.shape[-1]))
    return (final_memory, outputs)


def project(hidden, w_qkvz, w_beta_alpha):
    model_dim = hidden.shape[-1]
    flat_rows = hidden.reshape(-1, model_dim)
    projected = jnp.dot(
        flat_rows, w_qkvz.reshape(model_dim, -1), preferred_element_type=jnp.float32
    ).astype(jnp.bfloat16)
    gate_raw = jnp.dot(
        flat_rows, w_beta_alpha.reshape(model_dim, -1), preferred_element_type=jnp.float32
    ).astype(jnp.bfloat16)
    lead_shape = hidden.shape[:-1]
    return (
        projected.reshape(lead_shape + w_qkvz.shape[1:]),
        gate_raw.reshape(lead_shape + w_beta_alpha.shape[1:]),
    )


def advance(
    projected, gate_raw, lengths, memory, conv_state, conv_weight, decay_log, step_bias, norm_gain
):
    items = projected.shape[0]
    new_tokens = projected.shape[1]
    key_heads = projected.shape[2]
    value_heads = memory.shape[1]
    key_dim = memory.shape[2]
    value_dim = memory.shape[3]
    group_size = value_heads // key_heads
    channels = conv_state.shape[-1]
    tap_count = conv_weight.shape[0]
    mixed_part = projected[..., :channels]
    z_part = projected[..., channels:]
    extended = jnp.concatenate([conv_state, mixed_part], axis=1)
    convolved = jnp.zeros((items, new_tokens, key_heads, channels), jnp.float32)
    for offset in range(tap_count):
        convolved = convolved + conv_weight[offset].astype(jnp.float32) * extended[
            :, offset : offset + new_tokens
        ].astype(jnp.float32)
    activated = jax.nn.silu(convolved)
    tail_rows = jax.vmap(
        lambda rows_in, first_row: lax.dynamic_slice_in_dim(rows_in, first_row, tap_count - 1, 0)
    )(extended, lengths)
    queries = activated[..., :key_dim]
    queries = (
        queries
        * lax.rsqrt(jnp.sum(queries * queries, axis=-1, keepdims=True) + 1e-06)
        * (1.0 / math.sqrt(key_dim))
    )
    key_rows = activated[..., key_dim : 2 * key_dim]
    key_rows = key_rows * lax.rsqrt(jnp.sum(key_rows * key_rows, axis=-1, keepdims=True) + 1e-06)
    values = activated[..., 2 * key_dim :].reshape(items, new_tokens, value_heads, value_dim)
    queries = jnp.repeat(queries, group_size, axis=2)
    key_rows = jnp.repeat(key_rows, group_size, axis=2)
    gate_vals = gate_raw.astype(jnp.float32)
    beta_logit = gate_vals[..., :group_size].reshape(items, new_tokens, value_heads)
    decay_input = gate_vals[..., group_size:].reshape(items, new_tokens, value_heads)
    live_mask = jnp.arange(new_tokens, dtype=jnp.int32)[None, :] < lengths[:, None]
    beta_gate = jnp.where(live_mask[..., None], jax.nn.sigmoid(beta_logit), 0.0)
    decays = jnp.where(
        live_mask[..., None], -jnp.exp(decay_log) * jax.nn.softplus(decay_input + step_bias), 0.0
    )
    final_memory, core = delta_rule(
        memory,
        queries.transpose(0, 2, 1, 3),
        key_rows.transpose(0, 2, 1, 3),
        values.transpose(0, 2, 1, 3),
        decays.transpose(0, 2, 1),
        beta_gate.transpose(0, 2, 1),
    )
    core = core.transpose(0, 2, 1, 3)
    z_gate = z_part.astype(jnp.float32).reshape(items, new_tokens, value_heads, value_dim)
    normed = (
        core
        * lax.rsqrt(jnp.mean(core * core, axis=-1, keepdims=True) + 1e-06)
        * norm_gain
        * jax.nn.silu(z_gate)
    )
    normed = jnp.where(live_mask[..., None, None], normed, 0.0).astype(jnp.bfloat16)
    return (normed.reshape(items, new_tokens, value_heads * value_dim), final_memory, tail_rows)


def local(
    hidden,
    lengths,
    owners,
    slot_ids,
    state_cache,
    conv_cache,
    w_qkvz,
    w_beta_alpha,
    conv_weight,
    decay_log,
    step_bias,
    norm_gain,
    w_out,
):
    cache_count = lax.axis_size("cache")
    my_index = lax.axis_index("cache")
    conv_count = hidden.shape[0]
    slot_count = state_cache.shape[0]
    capacity = (slot_count + cache_count - 1) // cache_count
    owner_rows = owners.reshape(cache_count, conv_count)
    slot_rows = slot_ids.reshape(cache_count, conv_count)
    length_rows = lengths.reshape(cache_count, conv_count)
    owner_marks = (
        owner_rows[:, :, None] == jnp.arange(cache_count, dtype=jnp.int32)[None, None, :]
    ).astype(jnp.int32)
    rank_rows = jnp.sum((jnp.cumsum(owner_marks, axis=1) - owner_marks) * owner_marks, axis=2)
    places = jnp.arange(capacity, dtype=jnp.int32)
    served = (owner_rows == my_index)[:, None, :] & (rank_rows[:, None, :] == places[None, :, None])
    serve_slot = jnp.sum(jnp.where(served, slot_rows[:, None, :], 0), axis=2)
    serve_live = jnp.any(served, axis=2)
    target_rows = jnp.where(serve_live, serve_slot, slot_count).reshape(-1)
    my_owner = lax.dynamic_index_in_dim(owner_rows, my_index, 0, keepdims=False)
    my_rank = lax.dynamic_index_in_dim(rank_rows, my_index, 0, keepdims=False)
    my_lengths = lax.dynamic_index_in_dim(length_rows, my_index, 0, keepdims=False)
    pick_rows = my_owner * capacity + my_rank
    homeward = (
        my_owner[None, None, :] == jnp.arange(cache_count, dtype=jnp.int32)[:, None, None]
    ) & (my_rank[None, None, :] == places[None, :, None])
    back_index = jnp.sum(
        jnp.where(homeward, jnp.arange(conv_count, dtype=jnp.int32)[None, None, :], 0), axis=2
    ).reshape(-1)
    projected, gate_raw = project(hidden, w_qkvz, w_beta_alpha)
    lanes = (cache_count, capacity)
    fetched_memory, fetched_conv = (
        lax.all_to_all(state_cache[serve_slot], "cache", split_axis=0, concat_axis=0, tiled=True),
        lax.all_to_all(
            conv_cache[serve_slot].astype(jnp.float32),
            "cache",
            split_axis=0,
            concat_axis=0,
            tiled=True,
        ),
    )
    memories = fetched_memory.reshape((-1,) + state_cache.shape[1:])[pick_rows]
    conv_states = fetched_conv.reshape((-1,) + conv_cache.shape[1:])[pick_rows].astype(jnp.bfloat16)
    normed, final_memory, tail_rows = advance(
        projected,
        gate_raw,
        my_lengths,
        memories,
        conv_states,
        conv_weight,
        decay_log,
        step_bias,
        norm_gain,
    )
    outgoing = (
        final_memory[back_index].reshape(lanes + final_memory.shape[1:]),
        tail_rows[back_index].astype(jnp.float32).reshape(lanes + tail_rows.shape[1:]),
    )
    stored_memory, stored_conv = (
        lax.all_to_all(
            outgoing[0].astype(jnp.bfloat16), "cache", split_axis=0, concat_axis=0, tiled=True
        ).astype(jnp.float32),
        lax.all_to_all(
            outgoing[1].astype(jnp.bfloat16), "cache", split_axis=0, concat_axis=0, tiled=True
        ).astype(jnp.float32),
    )
    new_state_cache = state_cache.at[target_rows].set(
        stored_memory.reshape((-1,) + state_cache.shape[1:]), mode="drop"
    )
    new_conv_cache = conv_cache.at[target_rows].set(
        stored_conv.reshape((-1,) + conv_cache.shape[1:]).astype(jnp.bfloat16), mode="drop"
    )
    token_rows = normed.reshape(-1, normed.shape[-1])
    share = w_out.shape[1] // lax.axis_size("tensor")
    summed = lax.psum_scatter(
        lax.dot_general(
            w_out, token_rows, (((0,), (1,)), ((), ())), preferred_element_type=jnp.float32
        ),
        "tensor",
        scatter_dimension=0,
        tiled=True,
    )
    layer_out = summed.T.astype(jnp.bfloat16).reshape(conv_count, hidden.shape[1], share)
    return (layer_out, new_state_cache, new_conv_cache)


def solution(mesh):
    return jax.shard_map(
        local,
        mesh=mesh,
        in_specs=(
            P("cache", None, None),
            P(),
            P(),
            P(),
            P("cache", "tensor", None, None),
            P("cache", None, "tensor", None),
            P(None, "tensor", None),
            P(None, "tensor", None),
            P(None, "tensor", None),
            P("tensor"),
            P("tensor"),
            P(),
            P("tensor", None),
        ),
        out_specs=(
            P("cache", None, "tensor"),
            P("cache", "tensor", None, None),
            P("cache", None, "tensor", None),
        ),
        check_vma=False,
    )
```

profile of v0, /device:TPU:2, one launch (start us, length us, event | category | flops | bytes accessed | tf_op | source)
XLA Modules:
  0.0 212.2 jit_solution(8746498223825437665)
XLA Ops:
  7.2 3.3 %copy.257 = f32[16,2,128,128]{3,2,1,0:T(8,128)} copy(f32[16,2,128,128]{3,2,1,0:T(8,128)} %param.19) | data formatting | bytes 4194304
  14.3 7.5 %all-to-all-start.1 = ((bf16[16,2,768]{2,1,0:T(2,128)(2,1)}), bf16[16,2,768]{2,1,0:T(2,128)(2,1)S(1)}, u32[]{:S(2)}, u32[]{:S(2)}) async-start(bf16[16,2,768]{2,1,0:T(2,128)(2,1)} %reshape.661), calls=%async_computation.1 | async-start | bytes 98304 | tf_op jit(solution)/shard_map/all_to_all | solution.py:213
  22.0 3.5 %fusion.34 = f32[1,4,8,128]{3,1,2,0:T(4,128)S(1)} fusion(bf16[1024,2048]{1,0:T(8,128)(2,1)} %bitcast.277, bf16[2048,1,4]{0,2,1:T(4,128)(2,1)S(1)} %copy-done.13), kind=kOutput, calls=%fused_computation.72 | convolution fusion | flops 16785408 | bytes 4227072 | tf_op jit(solution)/shard_map/dot_general | solution.py:94
  25.6 3.4 %fusion.30 = bf16[1024,768]{1,0:T(8,128)(2,1)S(1)} fusion(bf16[1024,2048]{1,0:T(8,128)(2,1)S(1)} %bitcast.278, bf16[2048,1,768]{2,0,1:T(8,128)(2,1)S(1)} %copy-done), kind=kOutput, calls=%fused_computation.69 | convolution fusion | flops 3222011904 | bytes 8912896 | tf_op jit(solution)/shard_map/dot_general | solution.py:91
  33.8 2.5 %copy.193 = f32[8,128,1,256]{1,3,0,2:T(8,128)} copy(f32[8,128,1,256]{3,1,2,0:T(8,128)} %slice_convert_fusion) | data formatting | bytes 2097152 | tf_op jit(solution)/shard_map/reshape | solution.py:156
  36.4 2.6 %copy.195 = f32[8,128,2,128]{3,1,2,0:T(8,128)} copy(f32[8,128,2,128]{1,3,2,0:T(8,128)} %bitcast.280) | data formatting | bytes 2097152 | tf_op jit(solution)/shard_map/reshape | solution.py:156
  38.9 3.6 %gather_fusion = f32[16,2,128,128]{3,2,1,0:T(8,128)} fusion(f32[16,2,128,128]{3,2,1,0:T(8,128)} %copy.257, s32[1024]{0:T(1024)S(1)} %pad_clamp_fusion.2), kind=kCustom, calls=%fused_computation | custom fusion | bytes 4194368 | tf_op jit(solution)/shard_map/gather | solution.py:212
  42.5 7.4 %all-to-all-start = ((f32[16,1,2,128,128]{4,3,2,1,0:T(8,128)}), f32[16,1,2,128,128]{4,3,2,1,0:T(8,128)}, u32[]{:S(2)}, u32[]{:S(2)}) async-start(f32[16,1,2,128,128]{4,3,2,1,0:T(8,128)} %bitcast.276), calls=%async_computation | async-start | bytes 4194304 | tf_op jit(solution)/shard_map/all_to_all | solution.py:212
  50.7 3.7 %divide_multiply_fusion = f32[8,128,1,512]{3,1,2,0:T(8,128)S(1)} fusion(bf16[8,128,1,512]{3,1,2,0:T(8,128)(2,1)} %slice.88, bf16[8,3,1,512]{3,1,2,0:T(4,128)(2,1)S(1)} %copy.185, f32[512]{0:T(512)S(1)} %bitcast.303, f32[512]{0:T(512)S(1)} %bitcast.304, f32[512]{0:T(512)S(1)} %bitcast.302, f32[512]{0:T(512)S(1)} %bitcast.301), kind=kLoop, calls=%fused_computation.68 | loop fusion | flops 12582912 | bytes 3178496 | tf_op jit(solution)/shard_map/jit(silu)/mul | solution.py:124
  56.8 2.7 %reshape.555 = f32[8,128,2,128]{3,2,1,0:T(2,128)} reshape(f32[8,128,1,256]{3,1,2,0:T(8,128)} %slice.97) | data formatting | bytes 2097152 | tf_op jit(solution)/shard_map/reshape | solution.py:136
  64.8 11.8 %all-to-all-done = f32[16,1,2,128,128]{4,3,2,1,0:T(8,128)} async-done(((f32[16,1,2,128,128]{4,3,2,1,0:T(8,128)}), f32[16,1,2,128,128]{4,3,2,1,0:T(8,128)}, u32[]{:S(2)}, u32[]{:S(2)}) %all-to-all-start) | async-done | bytes 2097184 | tf_op jit(solution)/shard_map/all_to_all | solution.py:212
  76.6 3.2 %gather_fusion.1 = f32[8,2,128,128]{3,2,1,0:T(8,128)} fusion(f32[16,2,128,128]{3,2,1,0:T(8,128)} %bitcast.12, s32[1024]{0:T(1024)S(1)} %pad_clamp_fusion.1), kind=kCustom, calls=%fused_computation.1 | custom fusion | bytes 2097184 | tf_op jit(solution)/shard_map/gather | solution.py:221
  79.7 38.4 %while.12 = (s32[]{:T(128)}, f32[8,2,128,128]{3,2,1,0:T(8,128)}, f32[2,8,2,64,128]{4,3,0,2,1:T(8,128)}, f32[2,8,2,64]{3,0,1,2:T(2,128)S(1)}, f32[2,8,2,64,128]{4...) while((s32[]{:T(128)}, f32[8,2,128,128]{3,2,1,0:T(8,128)}, ...), condition=%wide.region_7.8_spmd, body=%wide.region_5.7_spmd.sunk | while | flops 1613382656 | bytes 52390600 | solution.py:72
  119.8 2.5 %fusion.42 = bf16[8,128,2,128]{3,1,2,0:T(8,128)(2,1)} fusion(f32[2,8,2,64,128]{4,3,0,2,1:T(8,128)} %get-tuple-element.46, f32[8,128,2,128]{3,1,2,0:T(8,128)} %copy.195, f32[128]{0:T(128)S(1)} %copy-done.19, f32[8,128,2]{1,2,0:T(2,128)S(1)} %add_rsqrt_fusion, pred[8,128]{1,0:T(8,128)(4,1)S(1)} %iota_compare_fusion.5), kind=kLoop, calls=%fused_computation.84 | loop fusion | flops 2359296 | bytes 2631168 | tf_op jit(solution)/shard_map/convert_element_type | solution.py:163
  124.4 5.9 %convolution_bitcast_fusion = f32[2048,1024]{0,1:T(8,128)} fusion(bf16[256,2048]{1,0:T(8,128)(2,1)} %param.27, bf16[32,8,8,128]{3,2,1,0:T(8,128)(2,1)} %bitcast.281), kind=kOutput, calls=%fused_computation.61 | convolution fusion | flops 1073741824 | bytes 9961472 | tf_op jit(solution)/shard_map/dot_general | solution.py:255
  132.0 3.8 %copy.197 = bf16[8,131,1,512]{3,2,0,1:T(2,128)(2,1)} copy(bf16[8,131,1,512]{3,1,2,0:T(8,128)(2,1)S(1)} %pad_maximum_fusion) | data formatting | bytes 2146304 | tf_op jit(solution)/shard_map/concatenate | solution.py:118
  138.5 6.6 %all-to-all-start.3 = ((bf16[16,1,3,1,512]{4,2,3,1,0:T(4,128)(2,1)}), bf16[16,1,3,1,512]{4,2,3,1,0:T(4,128)(2,1)S(1)}, u32[]{:S(2)}, u32[]{:S(2)}) async-start(bf16[16,1,3,1,512]{4,2,3,1,0:T(4,128)(2,1)} %bitcast.60), calls=%async_computation.4 | async-start | bytes 131072 | tf_op jit(solution)/shard_map/all_to_all | solution.py:242
  145.1 2.9 %gather_fusion.4 = bf16[16,2,128,128]{3,2,1,0:T(8,128)(2,1)} fusion(f32[8,2,128,128]{3,2,1,0:T(8,128)} %get-tuple-element.47, s32[1024]{0:T(1024)S(1)} %pad_clamp_fusion), kind=kCustom, calls=%fused_computation.4 | custom fusion | bytes 2097216 | tf_op jit(solution)/shard_map/gather | solution.py:235
  148.0 3.3 %all-to-all-done.3 = bf16[16,1,3,1,512]{4,2,3,1,0:T(4,128)(2,1)S(1)} async-done(((bf16[16,1,3,1,512]{4,2,3,1,0:T(4,128)(2,1)}), bf16[16,1,3,1,512]{4,2,3,1,0:T(4,128)(2,1)S(1)}, u32[]{:S(2)}, u32[]{:S(2)}) %all-to-all-start.3) | async-done | bytes 49184 | tf_op jit(solution)/shard_map/all_to_all | solution.py:242
  151.4 5.6 %all-to-all-start.2 = ((bf16[16,1,2,128,128]{4,3,2,1,0:T(8,128)(2,1)}), bf16[16,1,2,128,128]{4,3,2,1,0:T(8,128)(2,1)}, u32[]{:S(2)}, u32[]{:S(2)}) async-start(bf16[16,1,2,128,128]{4,3,2,1,0:T(8,128)(2,1)} %bitcast.279), calls=%async_computation.3 | async-start | bytes 2097152 | tf_op jit(solution)/shard_map/all_to_all | solution.py:239
  158.8 9.7 %all-to-all-done.2 = bf16[16,1,2,128,128]{4,3,2,1,0:T(8,128)(2,1)} async-done(((bf16[16,1,2,128,128]{4,3,2,1,0:T(8,128)(2,1)}), bf16[16,1,2,128,128]{4,3,2,1,0:T(8,128)(2,1)}, u32[]{:S(2)}, u32[]{:S(2)}) %all-to-all-start.2) | async-done | bytes 1048608 | tf_op jit(solution)/shard_map/all_to_all | solution.py:239
  168.5 2.9 %bitcast_convert_fusion = f32[16,2,128,128]{3,2,1,0:T(8,128)} fusion(bf16[16,1,2,128,128]{4,3,2,1,0:T(8,128)(2,1)} %all-to-all-done.2), kind=kLoop, calls=%fused_computation.77 | loop fusion | flops 524288 | bytes 3145728 | tf_op jit(solution)/shard_map/reshape | solution.py:247
  171.4 4.9 %scatter_fusion = f32[16,2,128,128]{3,2,1,0:T(8,128)} fusion(f32[16,2,128,128]{3,2,1,0:T(8,128)} %copy.257, s32[16]{0:T(128)S(1)} %fusion.61, f32[16,2,128,128]{3,2,1,0:T(8,128)} %bitcast_convert_fusion), kind=kCustom, calls=%fused_computation.7 | custom fusion | bytes 6291520 | tf_op jit(solution)/shard_map/scatter | solution.py:246
  176.3 27.4 %reduce-scatter.2.cloned.1.call-done = f32[128,1024]{0,1:T(8,128)} async-done(((f32[2048,1024]{0,1:T(8,128)}), f32[128,1024]{0,1:T(8,128)}) %reduce-scatter.2.cloned.1.call-update) | async-done | bytes 524304 | tf_op jit(solution)/shard_map/reduce_scatter | solution.py:254
  (183 shorter events, 66.6 us)
Async XLA Ops:
  7.2 18.4 %copy-start = (bf16[2048,1,768]{2,0,1:T(8,128)(2,1)S(1)}, bf16[2048,1,768]{2,0,1:T(8,128)(2,1)}, u32[]{:S(2)}) copy-start(bf16[2048,1,768]{2,0,1:T(8,128)(2,1)} %param.21) | copy-start | bytes 9437188
  7.2 14.6 %copy-start.18 = (s32[128]{0:T(128)S(1)}, s32[128]{0:T(128)}, u32[]{:S(2)}) copy-start(s32[128]{0:T(128)} %param.16) | copy-start | bytes 1540
  7.2 3.3 %copy-start.16 = (s32[128]{0:T(128)S(1)}, s32[128]{0:T(128)}, u32[]{:S(2)}) copy-start(s32[128]{0:T(128)} %param.17) | copy-start | bytes 1540
  7.2 3.5 %copy-start.17 = (s32[128]{0:T(128)S(1)}, s32[128]{0:T(128)}, u32[]{:S(2)}) copy-start(s32[128]{0:T(128)} %param.18) | copy-start | bytes 1540
  7.2 4.5 %copy-start.12 = (bf16[16,3,1,512]{3,0,2,1:T(8,128)(2,1)S(1)}, bf16[16,3,1,512]{3,0,2,1:T(8,128)(2,1)}, u32[]{:S(2)}) copy-start(bf16[16,3,1,512]{3,0,2,1:T(8,128)(2,1)} %param.20) | copy-start | bytes 147460
  7.2 14.8 %copy-start.13 = (bf16[2048,1,4]{0,2,1:T(4,128)(2,1)S(1)}, bf16[2048,1,4]{0,2,1:T(4,128)(2,1)}, u32[]{:S(2)}) copy-start(bf16[2048,1,4]{0,2,1:T(4,128)(2,1)} %param.22) | copy-start | bytes 49156
  7.2 14.6 %copy-start.20 = (f32[2]{0:T(128)S(1)}, f32[2]{0:T(128)}, u32[]{:S(2)}) copy-start(f32[2]{0:T(128)} %param.24) | copy-start | bytes 28
  14.3 28.2 %all-to-all-start.1 = ((bf16[16,2,768]{2,1,0:T(2,128)(2,1)}), bf16[16,2,768]{2,1,0:T(2,128)(2,1)S(1)}, u32[]{:S(2)}, u32[]{:S(2)}) async-start(bf16[16,2,768]{2,1,0:T(2,128)(2,1)} %reshape.661), calls=%async_computation.1 | async-start | bytes 98304 | tf_op jit(solution)/shard_map/all_to_all | solution.py:213
  22.0 3.5 %copy-start.8 = (bf16[8,128,2048]{2,1,0:T(8,128)(2,1)S(1)}, bf16[8,128,2048]{2,1,0:T(8,128)(2,1)}, u32[]{:S(2)}) copy-start(bf16[8,128,2048]{2,1,0:T(8,128)(2,1)} %param.15) | copy-start | bytes 12582916
  25.6 5.7 %copy-start.15 = (f32[2]{0:T(128)S(1)}, f32[2]{0:T(128)}, u32[]{:S(2)}) copy-start(f32[2]{0:T(128)} %param.25) | copy-start | bytes 28
  42.5 7.4 %copy-start.14 = (bf16[4,1,512]{2,0,1:T(4,128)(2,1)S(1)}, bf16[4,1,512]{2,0,1:T(4,128)(2,1)}, u32[]{:S(2)}) copy-start(bf16[4,1,512]{2,0,1:T(4,128)(2,1)} %param.23) | copy-start | bytes 12292
  42.5 34.1 %all-to-all-start = ((f32[16,1,2,128,128]{4,3,2,1,0:T(8,128)}), f32[16,1,2,128,128]{4,3,2,1,0:T(8,128)}, u32[]{:S(2)}, u32[]{:S(2)}) async-start(f32[16,1,2,128,128]{4,3,2,1,0:T(8,128)} %bitcast.276), calls=%async_computation | async-start | bytes 4194304 | tf_op jit(solution)/shard_map/all_to_all | solution.py:212
  49.9 153.8 %reduce-scatter.2.cloned.1.call-start = ((), (), s32[]{:S(2)}) async-start(), calls=%async_computation.5 | async-start | bytes 8912896 | tf_op jit(solution)/shard_map/reduce_scatter | solution.py:254
  59.5 2.5 %copy-start.6 = (f32[8,128,1,512]{3,1,2,0:T(8,128)S(1)}, f32[8,128,1,512]{3,1,2,0:T(8,128)}, u32[]{:S(2)}) copy-start(f32[8,128,1,512]{3,1,2,0:T(8,128)} %copy-done.5) | copy-start | bytes 6291460
  79.7 40.0 %copy-start.19 = (f32[128]{0:T(128)S(1)}, f32[128]{0:T(128)}, u32[]{:S(2)}) copy-start(f32[128]{0:T(128)} %param.26) | copy-start | bytes 1540
  80.5 2.4 %copy-start.3 = (f32[2,8,2,64,128]{4,3,2,1,0:T(8,128)S(1)}, f32[2,8,2,64,128]{4,3,2,1,0:T(8,128)}, u32[]{:S(2)}) copy-start(f32[2,8,2,64,128]{4,3,2,1,0:T(8,128)} %get-tuple-element.244) | copy-start | bytes 3145732 | tf_op jit(solution)/shard_map/while
  89.6 2.0 copy-start.7
  92.9 1.7 copy-start.4
  95.8 2.2 %copy-start.10 = (f32[2,8,2,64,128]{4,3,0,2,1:T(8,128)}, f32[2,8,2,64,128]{4,3,0,2,1:T(8,128)S(1)}, u32[]{:S(2)}) copy-start(f32[2,8,2,64,128]{4,3,0,2,1:T(8,128)S(1)} %fusion.189) | copy-start | bytes 3145732 | tf_op jit(solution)/shard_map/while
  99.8 2.4 %copy-start.3 = (f32[2,8,2,64,128]{4,3,2,1,0:T(8,128)S(1)}, f32[2,8,2,64,128]{4,3,2,1,0:T(8,128)}, u32[]{:S(2)}) copy-start(f32[2,8,2,64,128]{4,3,2,1,0:T(8,128)} %get-tuple-element.244) | copy-start | bytes 3145732 | tf_op jit(solution)/shard_map/while
  108.8 2.0 copy-start.7
  115.0 2.2 %copy-start.10 = (f32[2,8,2,64,128]{4,3,0,2,1:T(8,128)}, f32[2,8,2,64,128]{4,3,0,2,1:T(8,128)S(1)}, u32[]{:S(2)}) copy-start(f32[2,8,2,64,128]{4,3,0,2,1:T(8,128)S(1)} %fusion.189) | copy-start | bytes 3145732 | tf_op jit(solution)/shard_map/while
  138.5 12.9 %all-to-all-start.3 = ((bf16[16,1,3,1,512]{4,2,3,1,0:T(4,128)(2,1)}), bf16[16,1,3,1,512]{4,2,3,1,0:T(4,128)(2,1)S(1)}, u32[]{:S(2)}, u32[]{:S(2)}) async-start(bf16[16,1,3,1,512]{4,2,3,1,0:T(4,128)(2,1)} %bitcast.60), calls=%async_computation.4 | async-start | bytes 131072 | tf_op jit(solution)/shard_map/all_to_all | solution.py:242
  151.4 17.2 %all-to-all-start.2 = ((bf16[16,1,2,128,128]{4,3,2,1,0:T(8,128)(2,1)}), bf16[16,1,2,128,128]{4,3,2,1,0:T(8,128)(2,1)}, u32[]{:S(2)}, u32[]{:S(2)}) async-start(bf16[16,1,2,128,128]{4,3,2,1,0:T(8,128)(2,1)} %bitcast.279), calls=%async_computation.3 | async-start | bytes 2097152 | tf_op jit(solution)/shard_map/all_to_all | solution.py:239
  (9 other events, 12.4 us)
Sparse Core Ops, SparseCore 0:
  130.4 73.1 reduce-scatter.1
where the time goes:
time: 213 us; the launch traced here: 212 us
  local copies, waits for them, and re-layouts  52.3 us (25%)
  waiting for transfers between devices  52.3 us (25%)
  matrix products  46.2 us (22%)
  starting transfers between devices  27.1 us (13%)
  other arithmetic  19.4 us (9%)
  between operations  14.4 us (7%)
    reduce_scatter x1, waiting for transfers between devices, local(): lax.psum_scatter(lax.dot_general(w_out, token_rows, (((0,), (1,)), ((), (...  27.4 us
    all_to_all x1, waiting for transfers between devices, local(): lax.all_to_all(state_cache[serve_slot], 'cache', split_axis=0, concat_axi...  11.8 us
    all_to_all x1, waiting for transfers between devices, local(): lax.all_to_all(outgoing[0].astype(jnp.bfloat16), 'cache', split_axis=0, c...  9.74 us
    all_to_all x1, starting transfers between devices, local(): lax.all_to_all(conv_cache[serve_slot].astype(jnp.float32), 'cache', split...  7.48 us
    all_to_all x1, starting transfers between devices, local(): lax.all_to_all(state_cache[serve_slot], 'cache', split_axis=0, concat_axi...  7.36 us
    unnamed x34, local copies, waits for them, and re-layouts  7.23 us
    all_to_all x1, starting transfers between devices, local(): lax.all_to_all(outgoing[1].astype(jnp.bfloat16), 'cache', split_axis=0, c...  6.62 us
    dot_general x10, matrix products, unit_lower_inverse(): jnp.einsum('...ij,...jk->...ik', inverse, power, precision=HIGHEST_PREC)  6.48 us
  transfers between devices with their start and end apart: 5, of which 4 were waited for; matrix products, arithmetic and copies ran while one was open for 25% of the time, Pallas kernels for 0%

commit v1 on v0

v1 whole, which is shorter than its diff:
```python
import functools
import math

import jax
import jax.numpy as jnp
from jax import lax
from jax.experimental import pallas as pl
from jax.experimental.pallas import tpu as pltpu
from jax.sharding import PartitionSpec as P

F32, BF16 = jnp.float32, jnp.bfloat16
MESH = pl.DeviceIdType.MESH

NC = 16
NZ = 8
CONVS = 8
T = 128
DK = 128
CH = 512
SLOTS = 16
PAIR = 2


def mm(a, b, ca=1, cb=0):
    return lax.dot_general(
        a.astype(BF16), b.astype(BF16), (((ca,), (cb,)), ((), ())), preferred_element_type=F32
    )


def silu(v):
    return v * (0.5 * jnp.tanh(0.5 * v) + 0.5)


def kernel(
    hidden,
    lengths,
    owners,
    slots,
    state,
    conv_cache,
    w_qkvz,
    w_ba,
    conv_weight,
    decay_log,
    step_bias,
    norm_gain,
    w_out,
    layer_out,
    new_state,
    new_conv,
    convl,
    wbp,
    serve_slot,
    serve_live,
    cv_send,
    cv_recv,
    st_send,
    st_recv,
    ext,
    tail_tmp,
    wq,
    pk,
    u0,
    zg,
    eg_end,
    fin,
    nrm,
    rt_send,
    rt_recv,
    ybuf,
    cbuf,
    rsend,
    rrecv,
    newcf,
    cv_ss,
    cv_rs,
    st_ss,
    st_rs,
    rt_ss,
    rt_rs,
    co_ss,
    co_rs,
    ri_ss,
    ri_rs,
):
    me = lax.axis_index("cache")
    tt = lax.axis_index("tensor")
    z = tt // 2
    c = lax.rem(tt, 2)
    other = (me, z * 2 + 1 - c)
    up = (me, lax.rem(z + 1, NZ) * 2 + c)
    down = (me, lax.rem(z + NZ - 1, NZ) * 2 + c)

    barrier = pltpu.get_barrier_semaphore()

    def greet(d, carry):
        pl.semaphore_signal(barrier, inc=1, device_id=(lax.rem(me + d, NC), tt), device_id_type=MESH)
        return carry

    lax.fori_loop(1, NC, greet, 0)
    for peer in (other, up, down):
        pl.semaphore_signal(barrier, inc=1, device_id=peer, device_id_type=MESH)
    newcf[...] = conv_cache[...].astype(F32)
    convl[...] = jnp.zeros_like(convl)
    for s in range(SLOTS):
        for i in range(3):
            for b in range(4):
                convl[s, i * 4 + b : i * 4 + b + 1, :] = newcf[i, s : s + 1, b * 128 : (b + 1) * 128]
    wbp[...] = jnp.zeros_like(wbp)
    wbp[0:4, :] = w_ba[...].astype(F32)
    pl.semaphore_wait(barrier, NC - 1 + 3)

    def cv_copy(d):
        peer = lax.rem(me + d, NC)
        return pltpu.make_async_remote_copy(
            src_ref=cv_send.at[peer],
            dst_ref=cv_recv.at[me],
            send_sem=cv_ss.at[d],
            recv_sem=cv_rs.at[d],
            device_id=(peer, tt),
            device_id_type=MESH,
        )

    def st_copy(d):
        peer = lax.rem(me + d, NC)
        return pltpu.make_async_remote_copy(
            src_ref=st_send.at[peer],
            dst_ref=st_recv.at[me],
            send_sem=st_ss.at[d],
            recv_sem=st_rs.at[d],
            device_id=(peer, tt),
            device_id_type=MESH,
        )

    def conv_lane(peer):
        slot = jnp.int32(0)
        live = jnp.int32(0)
        for j in range(CONVS):
            hit = owners[peer * CONVS + j] == me
            slot = jnp.where(hit, slots[peer * CONVS + j], slot)
            live = jnp.where(hit, 1, live)
        serve_slot[peer] = slot
        serve_live[peer] = live
        return convl[slot].astype(BF16)

    tail_tmp[...] = jnp.zeros_like(tail_tmp)

    def send_conv(d, carry):
        peer = lax.rem(me + d, NC)
        cv_send[peer] = conv_lane(peer)
        cv_copy(d).start()
        return carry

    lax.fori_loop(1, NC, send_conv, 0)
    cv_recv[me] = conv_lane(me)

    def send_state(d, carry):
        peer = lax.rem(me + d, NC)
        st_send[peer] = state[serve_slot[peer]].astype(BF16)
        st_copy(d).start()
        return carry

    lax.fori_loop(1, NC, send_state, 0)
    st_recv[me] = state[serve_slot[me]].astype(BF16)

    def wait_conv(d, carry):
        cv_copy(d).wait()
        return carry

    lax.fori_loop(1, NC, wait_conv, 0)

    rows = lax.broadcasted_iota(jnp.int32, (T, T), 0)
    cols = lax.broadcasted_iota(jnp.int32, (T, T), 1)
    lane = lax.broadcasted_iota(jnp.int32, (1, T), 1)
    pos = lax.broadcasted_iota(jnp.int32, (T, 1), 0)

    def prepare(g, carry):
        x = hidden[pl.ds(g * PAIR, PAIR)].reshape(PAIR * T, hidden.shape[-1])
        projected = mm(x, w_qkvz[...]).astype(BF16)
        gates = mm(x, wbp[...], 1, 1).astype(BF16).astype(F32)
        rate = jnp.exp(
            jnp.where(lane == 2, decay_log[0], jnp.where(lane == 3, decay_log[1], 0.0))
        )
        bias = jnp.where(lane == 2, step_bias[0], jnp.where(lane == 3, step_bias[1], 0.0))
        inclusive = rows >= cols
        strictly = rows > cols
        tri = jnp.where(inclusive, 1.0, 0.0)
        chains = []
        for p in range(PAIR):
            j = g * PAIR + p
            length = lengths[me * CONVS + j]
            owner = owners[me * CONVS + j]
            live = pos < length
            mixed = projected[p * T : (p + 1) * T, :CH].astype(F32)
            z_part = projected[p * T : (p + 1) * T, CH:].astype(F32)
            held = cv_recv[owner].astype(F32)
            for i in range(3):
                for b in range(4):
                    ext[p, 5 + i : 6 + i, b * 128 : (b + 1) * 128] = held[i * 4 + b : i * 4 + b + 1, :]
            ext[p, 8 : 8 + T, :] = mixed
            convolved = conv_weight[3:4, :].astype(F32) * mixed
            for i in range(3):
                convolved = convolved + conv_weight[i : i + 1, :].astype(F32) * ext[p, 5 + i : 5 + i + T, :]
            for i in range(3):
                row = ext[p, pl.ds(5 + length + i, 1), :]
                for b in range(4):
                    tail_tmp[i * 4 + b : i * 4 + b + 1, :] = row[:, b * 128 : (b + 1) * 128]
            fin[j, 2 * DK : 2 * DK + 16, :] = tail_tmp[...].astype(BF16)
            act = silu(convolved)
            q = act[:, :DK]
            k = act[:, DK : 2 * DK]
            q = q * lax.rsqrt(jnp.sum(q * q, axis=-1, keepdims=True) + 1e-06) * (1.0 / math.sqrt(DK))
            k = k * lax.rsqrt(jnp.sum(k * k, axis=-1, keepdims=True) + 1e-06)
            zg[j] = jnp.where(
                live,
                silu(z_part) * jnp.concatenate([norm_gain[...], norm_gain[...]], axis=1),
                0.0,
            )
            raw = gates[p * T : (p + 1) * T, :]
            beta = jnp.where(live, 0.5 * jnp.tanh(0.5 * raw) + 0.5, 0.0)
            shifted = raw + bias
            decay = jnp.where(
                live,
                -rate * (jnp.maximum(shifted, 0.0) + jnp.log1p(jnp.exp(-jnp.abs(shifted)))),
                0.0,
            )
            total = jnp.dot(tri, decay, precision=lax.Precision.HIGHEST, preferred_element_type=F32)
            total_rows = total.T
            qk = mm(jnp.concatenate([k, q], axis=0), k, 1, 1)
            k_t = k.T
            for h in range(2):
                gc = total[:, 2 + h : 3 + h]
                gr = total_rows[2 + h : 3 + h, :]
                g_end = gr[:, T - 1 : T]
                bc = beta[:, h : h + 1]
                gap = jnp.where(inclusive, jnp.exp(jnp.where(inclusive, gc - gr, 0.0)), 0.0)
                lower = jnp.where(strictly, bc * qk[:T] * gap, 0.0)
                grow = jnp.exp(gc)
                wq[2 * j + h, T:, :] = (q * grow).astype(BF16)
                pk[2 * j + h, :T, :] = (qk[T:] * gap).astype(BF16)
                pk[2 * j + h, T:, :] = (k_t * jnp.exp(g_end - gr)).astype(BF16)
                eg_end[2 * j + h] = jnp.broadcast_to(jnp.exp(g_end), (8, T))
                right = jnp.concatenate(
                    [(bc * grow * k), bc * act[:, 2 * DK + h * T : 2 * DK + (h + 1) * T]], axis=1
                ).astype(BF16)
                chains.append((2 * j + h, lower, right))
        inverse = [
            jnp.where(rows == cols, 1.0, 0.0) - jnp.where(rows // 2 == cols // 2, low, 0.0)
            for _, low, _ in chains
        ]
        span = 2
        while span < T:
            block = (rows // (2 * span) == cols // (2 * span)) & (rows // span != cols // span)
            left = [mm(jnp.where(block, low, 0.0), inv) for (_, low, _), inv in zip(chains, inverse)]
            inverse = [inv - mm(inv, part) for inv, part in zip(inverse, left)]
            span *= 2
        for (at, _, right), inv in zip(chains, inverse):
            solved = mm(inv, right)
            wq[at, :T, :] = solved[:, :DK].astype(BF16)
            u0[at] = solved[:, DK:]
        return carry

    lax.fori_loop(0, CONVS // PAIR, prepare, 0)

    def wait_state(d, carry):
        st_copy(d).wait()
        return carry

    lax.fori_loop(1, NC, wait_state, 0)

    def finish(g, carry):
        for p in range(PAIR):
            j = g * PAIR + p
            owner = owners[me * CONVS + j]
            for h in range(2):
                at = 2 * j + h
                memory = st_recv[owner, h * DK : (h + 1) * DK, :]
                seen = mm(wq[at], memory)
                update = u0[at] - seen[:T]
                given = mm(pk[at], update)
                core = seen[T:] + given[:T]
                after = eg_end[at][0:1, :] * memory.astype(F32) + given[T:]
                fin[j, h * DK : (h + 1) * DK, :] = after.astype(BF16)
                scale = lax.rsqrt(jnp.mean(core * core, axis=-1, keepdims=True) + 1e-06)
                nrm[j, :, h * DK : (h + 1) * DK] = (
                    core * scale * zg[j, :, h * DK : (h + 1) * DK]
                ).astype(BF16)
        return carry

    lax.fori_loop(0, CONVS // PAIR, finish, 0)

    def rt_copy(d):
        peer = lax.rem(me + d, NC)
        return pltpu.make_async_remote_copy(
            src_ref=rt_send.at[peer],
            dst_ref=rt_recv.at[me],
            send_sem=rt_ss.at[d],
            recv_sem=rt_rs.at[d],
            device_id=(peer, tt),
            device_id_type=MESH,
        )

    def return_lane(peer):
        pick = jnp.int32(0)
        for j in range(CONVS):
            pick = jnp.where(owners[me * CONVS + j] == peer, j, pick)
        return fin[pick]

    def send_return(d, carry):
        peer = lax.rem(me + d, NC)
        rt_send[peer] = return_lane(peer)
        rt_copy(d).start()
        return carry

    lax.fori_loop(1, NC, send_return, 0)
    rt_recv[me] = return_lane(me)

    def core_copy(j):
        return pltpu.make_async_remote_copy(
            src_ref=ybuf.at[j, 1 - c],
            dst_ref=cbuf.at[j],
            send_sem=co_ss.at[j],
            recv_sem=co_rs.at[j],
            device_id=other,
            device_id_type=MESH,
        )

    def ring_copy(j, way, hop):
        if hop == 0:
            part = pl.ds(way * (T // 2), T // 2)
            src, dst = rsend.at[j, way, hop, part], rrecv.at[j, way, hop, part]
        else:
            src, dst = rsend.at[j, way, hop], rrecv.at[j, way, hop]
        return pltpu.make_async_remote_copy(
            src_ref=src,
            dst_ref=dst,
            send_sem=ri_ss.at[j, way, hop],
            recv_sem=ri_rs.at[j, way, hop],
            device_id=up if way == 0 else down,
            device_id_type=MESH,
        )

    def own_sum(j, dest):
        return ybuf[j, c, dest].astype(F32) + cbuf[j, dest].astype(F32)

    half = T // 2

    def turn(i, carry):
        @pl.when(i < CONVS)
        def _():
            normed = nrm[i]
            for n in range(NZ):
                y = mm(normed, w_out[:, n * 256 : (n + 1) * 256]).astype(BF16)
                ybuf[i, 0, n] = y[:, :128]
                ybuf[i, 1, n] = y[:, 128:]
            core_copy(i).start()

        @pl.when((i >= 1) & (i < CONVS + 1))
        def _():
            j = i - 1
            core_copy(j).wait()
            far = own_sum(j, lax.rem(z + 4, NZ)).astype(BF16)
            rsend[j, 0, 0, :half, :] = far[:half]
            rsend[j, 1, 0, half:, :] = far[half:]
            ring_copy(j, 0, 0).start()
            ring_copy(j, 1, 0).start()

        for hop in (1, 2, 3):

            @pl.when((i >= 1 + hop) & (i < CONVS + 1 + hop))
            def _(hop=hop):
                j = i - 1 - hop
                for way in (0, 1):
                    ring_copy(j, way, hop - 1).wait()
                    step = 4 - hop
                    dest = lax.rem(z + (step if way == 0 else NZ - step), NZ)
                    mine = own_sum(j, dest)
                    if hop == 1:
                        keep = slice(0, half) if way == 0 else slice(half, T)
                        alone = slice(half, T) if way == 0 else slice(0, half)
                        came = rrecv[j, way, 0, keep, :].astype(F32)
                        rsend[j, way, hop, keep, :] = (mine[keep] + came).astype(BF16)
                        rsend[j, way, hop, alone, :] = mine[alone].astype(BF16)
                    else:
                        came = rrecv[j, way, hop - 1].astype(F32)
                        rsend[j, way, hop] = (mine + came).astype(BF16)
                    ring_copy(j, way, hop).start()

        @pl.when(i >= 5)
        def _():
            j = i - 5
            ring_copy(j, 0, 3).wait()
            ring_copy(j, 1, 3).wait()
            total = own_sum(j, z) + rrecv[j, 0, 3].astype(F32) + rrecv[j, 1, 3].astype(F32)
            layer_out[j] = total.astype(BF16)

        return carry

    lax.fori_loop(0, CONVS + 5, turn, 0)

    def wait_return(d, carry):
        rt_copy(d).wait()
        return carry

    lax.fori_loop(1, NC, wait_return, 0)

    def store(s, carry):
        source = jnp.int32(0)
        found = jnp.int32(0)
        for d in range(NC):
            hit = (serve_slot[d] == s) & (serve_live[d] == 1)
            source = jnp.where(hit, d, source)
            found = jnp.where(hit, 1, found)
        came = rt_recv[source].astype(F32)
        fresh = found == 1
        new_state[s] = jnp.where(fresh, came[: 2 * DK], state[s])
        convl[s] = jnp.where(fresh, came[2 * DK :], convl[s])
        return carry

    lax.fori_loop(0, SLOTS, store, 0)
    for s in range(SLOTS):
        for i in range(3):
            for b in range(4):
                newcf[i, s : s + 1, b * 128 : (b + 1) * 128] = convl[s, i * 4 + b : i * 4 + b + 1, :]
    new_conv[...] = newcf[...].astype(BF16)


def local(
    hidden,
    lengths,
    owners,
    slot_ids,
    state_cache,
    conv_cache,
    w_qkvz,
    w_beta_alpha,
    conv_weight,
    decay_log,
    step_bias,
    norm_gain,
    w_out,
):
    vmem = pl.BlockSpec(memory_space=pltpu.VMEM)
    smem = pl.BlockSpec(memory_space=pltpu.SMEM)
    dma = pltpu.SemaphoreType.DMA
    layer_out, new_state, new_conv = pl.pallas_call(
        kernel,
        out_shape=(
            jax.ShapeDtypeStruct((CONVS, T, 128), BF16),
            jax.ShapeDtypeStruct((SLOTS, 2 * DK, T), F32),
            jax.ShapeDtypeStruct((3, SLOTS, CH), BF16),
        ),
        in_specs=[vmem, smem, smem, smem, vmem, vmem, vmem, vmem, vmem, smem, smem, vmem, vmem],
        out_specs=(vmem, vmem, vmem),
        scratch_shapes=[
            pltpu.VMEM((SLOTS, 16, 128), F32),
            pltpu.VMEM((128, 2048), F32),
            pltpu.SMEM((NC,), jnp.int32),
            pltpu.SMEM((NC,), jnp.int32),
            pltpu.VMEM((NC, 16, 128), BF16),
            pltpu.VMEM((NC, 16, 128), BF16),
            pltpu.VMEM((NC, 2 * DK, 128), BF16),
            pltpu.VMEM((NC, 2 * DK, 128), BF16),
            pltpu.VMEM((PAIR, 8 + T, CH), F32),
            pltpu.VMEM((16, 128), F32),
            pltpu.VMEM((2 * CONVS, 2 * T, DK), BF16),
            pltpu.VMEM((2 * CONVS, 2 * T, DK), BF16),
            pltpu.VMEM((2 * CONVS, T, DK), F32),
            pltpu.VMEM((CONVS, T, 2 * DK), F32),
            pltpu.VMEM((2 * CONVS, 8, 128), F32),
            pltpu.VMEM((CONVS, 2 * DK + 16, 128), BF16),
            pltpu.VMEM((CONVS, T, 2 * DK), BF16),
            pltpu.VMEM((NC, 2 * DK + 16, 128), BF16),
            pltpu.VMEM((NC, 2 * DK + 16, 128), BF16),
            pltpu.VMEM((CONVS, 2, NZ, T, 128), BF16),
            pltpu.VMEM((CONVS, NZ, T, 128), BF16),
            pltpu.VMEM((CONVS, 2, 4, T, 128), BF16),
            pltpu.VMEM((CONVS, 2, 4, T, 128), BF16),
            pltpu.VMEM((3, SLOTS, CH), F32),
            dma((NC,)),
            dma((NC,)),
            dma((NC,)),
            dma((NC,)),
            dma((NC,)),
            dma((NC,)),
            dma((CONVS,)),
            dma((CONVS,)),
            dma((CONVS, 2, 4)),
            dma((CONVS, 2, 4)),
        ],
        compiler_params=pltpu.CompilerParams(
            collective_id=0, has_side_effects=True, vmem_limit_bytes=56 * 1024 * 1024
        ),
    )(
        hidden,
        lengths,
        owners,
        slot_ids,
        state_cache.reshape(SLOTS, 2 * DK, 128),
        conv_cache.transpose(1, 2, 0, 3).reshape(3, SLOTS, CH),
        w_qkvz.reshape(2048, 768),
        w_beta_alpha.transpose(1, 2, 0).reshape(4, 2048),
        conv_weight.reshape(4, CH),
        decay_log,
        step_bias,
        norm_gain.reshape(1, 128),
        w_out,
    )
    return (
        layer_out,
        new_state.reshape(state_cache.shape),
        new_conv.reshape(3, 1, SLOTS, CH).transpose(2, 0, 1, 3),
    )


def solution(mesh):
    return jax.shard_map(
        local,
        mesh=mesh,
        in_specs=(
            P("cache", None, None),
            P(),
            P(),
            P(),
            P("cache", "tensor", None, None),
            P("cache", None, "tensor", None),
            P(None, "tensor", None),
            P(None, "tensor", None),
            P(None, "tensor", None),
            P("tensor"),
            P("tensor"),
            P(),
            P("tensor", None),
        ),
        out_specs=(
            P("cache", None, "tensor"),
            P("cache", "tensor", None, None),
            P("cache", None, "tensor", None),
        ),
        check_vma=False,
    )
```

time: 213 us -> 89.9 us (0.42)
  Pallas kernels: 0 us -> 83.6 us
  waiting for transfers between devices: 52.3 us -> 0 us
  local copies, waits for them, and re-layouts: 52.3 us -> 5.44 us
  matrix products: 46.2 us -> 0 us
  starting transfers between devices: 27.1 us -> 0 us
  other arithmetic: 19.4 us -> 0 us
  between operations: 14.4 us -> 0.65 us
    pallas_call x0 -> x1, Pallas kernels: none -> 83.6 us  [local(): pl.pallas_call(kernel, out_shape=(jax.ShapeDtypeStruct((CONVS, T, 128), B...]
    dot_general x37 -> x0, matrix products: 46.2 us -> none  [the longest x10 6.48 us: unit_lower_inverse(): jnp.einsum('...ij,...jk->...ik', inverse, power, precision=HIGHEST_PREC)]
    reduce_scatter x1 -> x0, waiting for transfers between devices: 27.4 us -> none  [local(): lax.psum_scatter(lax.dot_general(w_out, token_rows, (((0,), (1,)), ((), (...]
    all_to_all x4 -> x0, starting transfers between devices: 27 us -> none  [the longest x1 7.48 us: local(): lax.all_to_all(conv_cache[serve_slot].astype(jnp.float32), 'cache', split...]
    all_to_all x4 -> x0, waiting for transfers between devices: 24.9 us -> none  [the longest x1 11.8 us: local(): lax.all_to_all(state_cache[serve_slot], 'cache', split_axis=0, concat_axi...]
    gather x9 -> x0, local copies, waits for them, and re-layouts: 13.5 us -> none  [the longest x1 3.58 us: local(): state_cache[serve_slot]]
    reshape x8 -> x0, local copies, waits for them, and re-layouts: 10.5 us -> none  [the longest x2 5.17 us: advance(): activated[..., 2 * key_dim:]]
    scatter x2 -> x0, local copies, waits for them, and re-layouts: 5.96 us -> none  [the longest x1 4.9 us: local(): state_cache.at[target_rows]]
  transfers between devices with their start and end apart: 5 -> 0, of which waited for: 4 -> 0; matrix products, arithmetic and copies ran while one was open for 25% -> 0% of each run, Pallas kernels for 0% -> 0%
where the time goes in v1:
time: 89.9 us; the launch traced here: 89.7 us
  Pallas kernels  83.6 us (93%)
  local copies, waits for them, and re-layouts  5.44 us (6%)
    pallas_call x1, Pallas kernels, local(): pl.pallas_call(kernel, out_shape=(jax.ShapeDtypeStruct((CONVS, T, 128), B...  83.6 us
    unnamed x5, local copies, waits for them, and re-layouts  5.44 us

profile of v1, /device:TPU:2, one launch (start us, length us, event | category | flops | bytes accessed | tf_op | source)
XLA Modules:
  0.0 89.7 jit_solution(7911856038362597702)
XLA Ops:
  0.6 83.6 %shard_map.148 = (bf16[8,128,128]{2,1,0:T(8,128)(2,1)}, f32[16,256,128]{2,1,0:T(8,128)}, bf16[3,16,512]{2,1,0:T(8,128)(2,1)}) custom-call(bf16[8,128,2048]{2,1,0:T(8,128)(2,1)} %hidden.1, s32[128]{0:T(128)} %lengths.1, s32[128]{0:T(128)} %owners.1, s32[128]{0:T(128)} %slots.1, f32[16,256,128]{2,1,0:T(8,128)} %bitcast.20, bf16[3,16,512]{2,1,0:T(8,128)(2,1)} %bitcast.21, ...), custom_call_target="tpu_custom_call" | custom-call | tf_op jit(solution)/shard_map/pallas_call | solution.py:446
  84.3 1.7 %copy.21 = bf16[8,128,128]{2,1,0:T(8,128)(2,1)} copy(bf16[8,128,128]{2,1,0:T(8,128)(2,1)} %get-tuple-element.15) | data formatting | bytes 524288
  85.9 0.0 copy-start
  86.0 3.1 %copy.22 = f32[16,2,128,128]{3,2,1,0:T(8,128)} copy(f32[16,2,128,128]{3,2,1,0:T(8,128)} %bitcast.19) | data formatting | bytes 4194304
  89.1 0.0 copy-done
  89.1 0.6 copy.23
Async XLA Ops:
  85.9 3.1 %copy-start = (bf16[3,16,512]{2,1,0:T(8,128)(2,1)S(1)}, bf16[3,16,512]{2,1,0:T(8,128)(2,1)}, u32[]{:S(2)}) copy-start(bf16[3,16,512]{2,1,0:T(8,128)(2,1)} %get-tuple-element.8) | copy-start | bytes 147460

commit v2 on v1

--- a/solution.py
+++ b/solution.py
@@ -32,22 +32,29 @@
 
 
 def kernel(
-    hidden,
+    hidden_in,
     lengths,
     owners,
     slots,
-    state,
+    state_in,
     conv_cache,
-    w_qkvz,
+    w_qkvz_in,
     w_ba,
     conv_weight,
     decay_log,
     step_bias,
     norm_gain,
+    w_out_in,
+    layer_out,
+    new_state_out,
+    new_conv,
+    hidden,
+    state,
+    w_qkvz,
     w_out,
-    layer_out,
     new_state,
-    new_conv,
+    in_s,
+    out_s,
     convl,
     wbp,
     serve_slot,
@@ -91,6 +98,15 @@
     up = (me, lax.rem(z + 1, NZ) * 2 + c)
     down = (me, lax.rem(z + NZ - 1, NZ) * 2 + c)
 
+    loads = [
+        pltpu.make_async_copy(src, dst, in_s.at[n])
+        for n, (src, dst) in enumerate(
+            [(state_in, state), (w_qkvz_in, w_qkvz), (hidden_in, hidden), (w_out_in, w_out)]
+        )
+    ]
+    for load in loads:
+        load.start()
+
     barrier = pltpu.get_barrier_semaphore()
 
     def greet(d, carry):
@@ -154,13 +170,14 @@
     lax.fori_loop(1, NC, send_conv, 0)
     cv_recv[me] = conv_lane(me)
 
-    def send_state(d, carry):
+    loads[0].wait()
+
+    def pack_state(d, carry):
         peer = lax.rem(me + d, NC)
         st_send[peer] = state[serve_slot[peer]].astype(BF16)
-        st_copy(d).start()
-        return carry
-
-    lax.fori_loop(1, NC, send_state, 0)
+        return carry
+
+    lax.fori_loop(1, NC, pack_state, 0)
     st_recv[me] = state[serve_slot[me]].astype(BF16)
 
     def wait_conv(d, carry):
@@ -168,6 +185,14 @@
         return carry
 
     lax.fori_loop(1, NC, wait_conv, 0)
+
+    def send_state(d, carry):
+        st_copy(d).start()
+        return carry
+
+    lax.fori_loop(1, NC, send_state, 0)
+    loads[1].wait()
+    loads[2].wait()
 
     rows = lax.broadcasted_iota(jnp.int32, (T, T), 0)
     cols = lax.broadcasted_iota(jnp.int32, (T, T), 1)
@@ -287,8 +312,6 @@
                 ).astype(BF16)
         return carry
 
-    lax.fori_loop(0, CONVS // PAIR, finish, 0)
-
     def rt_copy(d):
         peer = lax.rem(me + d, NC)
         return pltpu.make_async_remote_copy(
@@ -311,9 +334,6 @@
         rt_send[peer] = return_lane(peer)
         rt_copy(d).start()
         return carry
-
-    lax.fori_loop(1, NC, send_return, 0)
-    rt_recv[me] = return_lane(me)
 
     def core_copy(j):
         return pltpu.make_async_remote_copy(
@@ -345,7 +365,36 @@
 
     half = T // 2
 
+    def far_hop(j):
+        core_copy(j).wait()
+        far = own_sum(j, lax.rem(z + 4, NZ)).astype(BF16)
+        rsend[j, 0, 0, :half, :] = far[:half]
+        rsend[j, 1, 0, half:, :] = far[half:]
+        ring_copy(j, 0, 0).start()
+        ring_copy(j, 1, 0).start()
+
+    def next_hop(j, hop):
+        for way in (0, 1):
+            ring_copy(j, way, hop - 1).wait()
+            step = 4 - hop
+            dest = lax.rem(z + (step if way == 0 else NZ - step), NZ)
+            mine = own_sum(j, dest)
+            if hop == 1:
+                keep = slice(0, half) if way == 0 else slice(half, T)
+                alone = slice(half, T) if way == 0 else slice(0, half)
+                came = rrecv[j, way, 0, keep, :].astype(F32)
+                rsend[j, way, hop, keep, :] = (mine[keep] + came).astype(BF16)
+                rsend[j, way, hop, alone, :] = mine[alone].astype(BF16)
+            else:
+                came = rrecv[j, way, hop - 1].astype(F32)
+                rsend[j, way, hop] = (mine + came).astype(BF16)
+            ring_copy(j, way, hop).start()
+
     def turn(i, carry):
+        @pl.when(i < CONVS // PAIR)
+        def _():
+            finish(i, 0)
+
         @pl.when(i < CONVS)
         def _():
             normed = nrm[i]
@@ -355,54 +404,37 @@
                 ybuf[i, 1, n] = y[:, 128:]
             core_copy(i).start()
 
-        @pl.when((i >= 1) & (i < CONVS + 1))
+        @pl.when(i >= 1)
         def _():
-            j = i - 1
-            core_copy(j).wait()
-            far = own_sum(j, lax.rem(z + 4, NZ)).astype(BF16)
-            rsend[j, 0, 0, :half, :] = far[:half]
-            rsend[j, 1, 0, half:, :] = far[half:]
-            ring_copy(j, 0, 0).start()
-            ring_copy(j, 1, 0).start()
-
-        for hop in (1, 2, 3):
-
-            @pl.when((i >= 1 + hop) & (i < CONVS + 1 + hop))
-            def _(hop=hop):
-                j = i - 1 - hop
-                for way in (0, 1):
-                    ring_copy(j, way, hop - 1).wait()
-                    step = 4 - hop
-                    dest = lax.rem(z + (step if way == 0 else NZ - step), NZ)
-                    mine = own_sum(j, dest)
-                    if hop == 1:
-                        keep = slice(0, half) if way == 0 else slice(half, T)
-                        alone = slice(half, T) if way == 0 else slice(0, half)
-                        came = rrecv[j, way, 0, keep, :].astype(F32)
-                        rsend[j, way, hop, keep, :] = (mine[keep] + came).astype(BF16)
-                        rsend[j, way, hop, alone, :] = mine[alone].astype(BF16)
-                    else:
-                        came = rrecv[j, way, hop - 1].astype(F32)
-                        rsend[j, way, hop] = (mine + came).astype(BF16)
-                    ring_copy(j, way, hop).start()
-
-        @pl.when(i >= 5)
+            far_hop(i - 1)
+
+        @pl.when(i >= 3)
         def _():
-            j = i - 5
-            ring_copy(j, 0, 3).wait()
-            ring_copy(j, 1, 3).wait()
-            total = own_sum(j, z) + rrecv[j, 0, 3].astype(F32) + rrecv[j, 1, 3].astype(F32)
-            layer_out[j] = total.astype(BF16)
-
-        return carry
-
-    lax.fori_loop(0, CONVS + 5, turn, 0)
+            next_hop(i - 3, 1)
+
+        return carry
+
+    loads[3].wait()
+    lax.fori_loop(0, CONVS // PAIR, turn, 0)
+    lax.fori_loop(1, NC, send_return, 0)
+    rt_recv[me] = return_lane(me)
+    lax.fori_loop(CONVS // PAIR, CONVS + 1, turn, 0)
+    for hop, first in ((1, CONVS - 2), (2, 0), (3, 0)):
+
+        def hops(j, carry, hop=hop):
+            next_hop(j, hop)
+            return carry
+
+        lax.fori_loop(first, CONVS, hops, 0)
 
     def wait_return(d, carry):
         rt_copy(d).wait()
         return carry
 
     lax.fori_loop(1, NC, wait_return, 0)
+
+    def leave(s):
+        return pltpu.make_async_copy(new_state.at[s], new_state_out.at[s], out_s.at[s])
 
     def store(s, carry):
         source = jnp.int32(0)
@@ -415,6 +447,7 @@
         fresh = found == 1
         new_state[s] = jnp.where(fresh, came[: 2 * DK], state[s])
         convl[s] = jnp.where(fresh, came[2 * DK :], convl[s])
+        leave(s).start()
         return carry
 
     lax.fori_loop(0, SLOTS, store, 0)
@@ -423,6 +456,37 @@
             for b in range(4):
                 newcf[i, s : s + 1, b * 128 : (b + 1) * 128] = convl[s, i * 4 + b : i * 4 + b + 1, :]
     new_conv[...] = newcf[...].astype(BF16)
+
+    def last(j, carry):
+        ring_copy(j, 0, 3).wait()
+        ring_copy(j, 1, 3).wait()
+        total = own_sum(j, z) + rrecv[j, 0, 3].astype(F32) + rrecv[j, 1, 3].astype(F32)
+        layer_out[j] = total.astype(BF16)
+        return carry
+
+    lax.fori_loop(0, CONVS, last, 0)
+
+    def left(s, carry):
+        leave(s).wait()
+        return carry
+
+    lax.fori_loop(0, SLOTS, left, 0)
+
+
+def hand_on(layer_in, state_in, conv_in, layer_out, state_out, conv_out, layer, state, conv, came, gone):
+    parts = [(layer_in, layer, layer_out), (conv_in, conv, conv_out)]
+    for n in range(8):
+        part = pl.ds(2 * n, 2)
+        parts.append((state_in.at[part], state.at[part], state_out.at[part]))
+    take = [pltpu.make_async_copy(a, b, came.at[n]) for n, (a, b, _) in enumerate(parts)]
+    give = [pltpu.make_async_copy(b, c, gone.at[n]) for n, (_, b, c) in enumerate(parts)]
+    for copy in take:
+        copy.start()
+    for here, there in zip(take, give):
+        here.wait()
+        there.start()
+    for copy in give:
+        copy.wait()
 
 
 def local(
@@ -443,16 +507,26 @@
     vmem = pl.BlockSpec(memory_space=pltpu.VMEM)
     smem = pl.BlockSpec(memory_space=pltpu.SMEM)
     dma = pltpu.SemaphoreType.DMA
-    layer_out, new_state, new_conv = pl.pallas_call(
+    far = pl.BlockSpec(memory_space=pl.ANY)
+    hbm = pl.BlockSpec(memory_space=pltpu.HBM)
+    results = (
+        jax.ShapeDtypeStruct((CONVS, T, 128), BF16),
+        jax.ShapeDtypeStruct((SLOTS, 2 * DK, T), F32),
+        jax.ShapeDtypeStruct((3, SLOTS, CH), BF16),
+    )
+    worked = pl.pallas_call(
         kernel,
-        out_shape=(
-            jax.ShapeDtypeStruct((CONVS, T, 128), BF16),
-            jax.ShapeDtypeStruct((SLOTS, 2 * DK, T), F32),
-            jax.ShapeDtypeStruct((3, SLOTS, CH), BF16),
-        ),
-        in_specs=[vmem, smem, smem, smem, vmem, vmem, vmem, vmem, vmem, smem, smem, vmem, vmem],
-        out_specs=(vmem, vmem, vmem),
+        out_shape=results,
+        in_specs=[far, smem, smem, smem, far, vmem, far, vmem, vmem, smem, smem, vmem, far],
+        out_specs=(vmem, far, vmem),
         scratch_shapes=[
+            pltpu.VMEM((CONVS, T, 2048), BF16),
+            pltpu.VMEM((SLOTS, 2 * DK, 128), F32),
+            pltpu.VMEM((2048, 768), BF16),
+            pltpu.VMEM((256, 2048), BF16),
+            pltpu.VMEM((SLOTS, 2 * DK, 128), F32),
+            dma((4,)),
+            dma((SLOTS,)),
             pltpu.VMEM((SLOTS, 16, 128), F32),
             pltpu.VMEM((128, 2048), F32),
             pltpu.SMEM((NC,), jnp.int32),
@@ -506,6 +580,13 @@
         norm_gain.reshape(1, 128),
         w_out,
     )
+    layer_out, new_state, new_conv = pl.pallas_call(
+        hand_on,
+        out_shape=results,
+        in_specs=[hbm, hbm, hbm],
+        out_specs=(hbm, hbm, hbm),
+        scratch_shapes=[pltpu.VMEM(r.shape, r.dtype) for r in results] + [dma((10,)), dma((10,))],
+    )(*worked)
     return (
         layer_out,
         new_state.reshape(state_cache.shape),

time: 89.9 us -> 65.2 us (0.73); the launches traced: 89.7 us -> 64.1 us
  Pallas kernels: 83.6 us -> 63.4 us
  local copies, waits for them, and re-layouts: 5.44 us -> 0 us
    pallas_call x1 -> x2, Pallas kernels: 83.6 us -> 63.4 us  [the longest x1 60.9 us: local(): pl.pallas_call(kernel, out_shape=results, in_specs=[far, smem, smem, smem...]
    unnamed x5 -> x0, local copies, waits for them, and re-layouts: 5.44 us -> none
where the time goes in v2:
time: 65.2 us; the launch traced here: 64.1 us
  Pallas kernels  63.4 us (97%)
    pallas_call x1, Pallas kernels, local(): pl.pallas_call(kernel, out_shape=results, in_specs=[far, smem, smem, smem...  60.9 us
    pallas_call x1, Pallas kernels, local(): pl.pallas_call(hand_on, out_shape=results, in_specs=[hbm, hbm, hbm], out_...  2.54 us

profile of v2, /device:TPU:2, one launch (start us, length us, event | category | flops | bytes accessed | tf_op | source)
XLA Modules:
  0.0 64.1 jit_solution(11940379946899841779)
XLA Ops:
  0.6 60.9 %shard_map.148 = (bf16[8,128,128]{2,1,0:T(8,128)(2,1)}, f32[16,256,128]{2,1,0:T(8,128)}, bf16[3,16,512]{2,1,0:T(8,128)(2,1)}) custom-call(bf16[8,128,2048]{2,1,0:T(8,128)(2,1)} %hidden_in.1, s32[128]{0:T(128)} %lengths.1, s32[128]{0:T(128)} %owners.1, s32[128]{0:T(128)} %slots.1, f32[16,256,128]{2,1,0:T(8,128)} %bitcast.19, bf16[3,16,512]{2,1,0:T(8,128)(2,1)} %bitcast.20, ...), custom_call_target="tpu_custom_call" | custom-call | tf_op jit(solution)/shard_map/pallas_call | solution.py:517
  61.5 2.5 %shard_map.149 = (bf16[8,128,128]{2,1,0:T(8,128)(2,1)}, f32[16,256,128]{2,1,0:T(8,128)}, bf16[3,16,512]{2,1,0:T(8,128)(2,1)}) custom-call(bf16[8,128,128]{2,1,0:T(8,128)(2,1)} %get-tuple-element.9.layer_in, f32[16,256,128]{2,1,0:T(8,128)} %get-tuple-element.10.state_in, bf16[3,16,512]{2,1,0:T(8,128)(2,1)} %get-tuple-element.11.conv_in), custom_call_target="tpu_custom_call" | custom-call | tf_op jit(solution)/shard_map/pallas_call | solution.py:583

commit v3 on v2

--- a/solution.py
+++ b/solution.py
@@ -19,6 +19,9 @@
 CH = 512
 SLOTS = 16
 PAIR = 2
+STEP = 2
+PREP = 4
+ORDER = sorted(range(1, NC), key=lambda n: -(min(n // 4, 4 - n // 4) + min(n % 4, 4 - n % 4)))
 
 
 def mm(a, b, ca=1, cb=0):
@@ -57,6 +60,8 @@
     out_s,
     convl,
     wbp,
+    proj,
+    gate,
     serve_slot,
     serve_live,
     cv_send,
@@ -74,8 +79,9 @@
     nrm,
     rt_send,
     rt_recv,
+    nrm_other,
+    w_pair,
     ybuf,
-    cbuf,
     rsend,
     rrecv,
     newcf,
@@ -85,6 +91,8 @@
     st_rs,
     rt_ss,
     rt_rs,
+    nx_ss,
+    nx_rs,
     co_ss,
     co_rs,
     ri_ss,
@@ -98,10 +106,13 @@
     up = (me, lax.rem(z + 1, NZ) * 2 + c)
     down = (me, lax.rem(z + NZ - 1, NZ) * 2 + c)
 
+    def ahead(n):
+        return lax.rem(me // 4 + n // 4, 4) * 4 + lax.rem(lax.rem(me, 4) + lax.rem(n, 4), 4)
+
     loads = [
         pltpu.make_async_copy(src, dst, in_s.at[n])
         for n, (src, dst) in enumerate(
-            [(state_in, state), (w_qkvz_in, w_qkvz), (hidden_in, hidden), (w_out_in, w_out)]
+            [(state_in, state), (w_out_in, w_out), (w_qkvz_in, w_qkvz), (hidden_in, hidden)]
         )
     ]
     for load in loads:
@@ -110,7 +121,7 @@
     barrier = pltpu.get_barrier_semaphore()
 
     def greet(d, carry):
-        pl.semaphore_signal(barrier, inc=1, device_id=(lax.rem(me + d, NC), tt), device_id_type=MESH)
+        pl.semaphore_signal(barrier, inc=1, device_id=(ahead(d), tt), device_id_type=MESH)
         return carry
 
     lax.fori_loop(1, NC, greet, 0)
@@ -122,12 +133,10 @@
         for i in range(3):
             for b in range(4):
                 convl[s, i * 4 + b : i * 4 + b + 1, :] = newcf[i, s : s + 1, b * 128 : (b + 1) * 128]
-    wbp[...] = jnp.zeros_like(wbp)
-    wbp[0:4, :] = w_ba[...].astype(F32)
     pl.semaphore_wait(barrier, NC - 1 + 3)
 
     def cv_copy(d):
-        peer = lax.rem(me + d, NC)
+        peer = ahead(d)
         return pltpu.make_async_remote_copy(
             src_ref=cv_send.at[peer],
             dst_ref=cv_recv.at[me],
@@ -138,7 +147,7 @@
         )
 
     def st_copy(d):
-        peer = lax.rem(me + d, NC)
+        peer = ahead(d)
         return pltpu.make_async_remote_copy(
             src_ref=st_send.at[peer],
             dst_ref=st_recv.at[me],
@@ -162,7 +171,7 @@
     tail_tmp[...] = jnp.zeros_like(tail_tmp)
 
     def send_conv(d, carry):
-        peer = lax.rem(me + d, NC)
+        peer = ahead(d)
         cv_send[peer] = conv_lane(peer)
         cv_copy(d).start()
         return carry
@@ -172,13 +181,29 @@
 
     loads[0].wait()
 
-    def pack_state(d, carry):
-        peer = lax.rem(me + d, NC)
+    for d in ORDER:
+        peer = ahead(d)
         st_send[peer] = state[serve_slot[peer]].astype(BF16)
-        return carry
-
-    lax.fori_loop(1, NC, pack_state, 0)
     st_recv[me] = state[serve_slot[me]].astype(BF16)
+
+    def columns(r, core):
+        return pl.ds(pl.multiple_of((lax.rem(z + 4 + r, NZ) * 2 + core) * 128, 128), 128)
+
+    def weight_copy(r):
+        return pltpu.make_async_remote_copy(
+            src_ref=w_out.at[:, columns(r, 1 - c)],
+            dst_ref=w_pair.at[pl.ds(256, 256), pl.ds(r * 128, 128)],
+            send_sem=co_ss.at[r],
+            recv_sem=co_rs.at[r],
+            device_id=other,
+            device_id_type=MESH,
+        )
+
+    loads[1].wait()
+    for r in range(NZ):
+        weight_copy(r).start()
+    for r in range(NZ):
+        w_pair[0:256, r * 128 : (r + 1) * 128] = w_out[:, columns(r, c)]
 
     def wait_conv(d, carry):
         cv_copy(d).wait()
@@ -186,13 +211,24 @@
 
     lax.fori_loop(1, NC, wait_conv, 0)
 
-    def send_state(d, carry):
+    for d in ORDER:
         st_copy(d).start()
-        return carry
-
-    lax.fori_loop(1, NC, send_state, 0)
-    loads[1].wait()
+
+    wbp[...] = jnp.zeros_like(wbp)
+    wbp[0:4, :] = w_ba[...].astype(F32)
     loads[2].wait()
+    loads[3].wait()
+
+    def project(g, carry):
+        x = hidden[pl.ds(g * STEP, STEP)].reshape(STEP * T, hidden.shape[-1])
+        projected = mm(x, w_qkvz[...]).astype(BF16)
+        gates = mm(x, wbp[...], 1, 1).astype(BF16).astype(F32)
+        for p in range(STEP):
+            proj[g * STEP + p] = projected[p * T : (p + 1) * T]
+            gate[g * STEP + p] = gates[p * T : (p + 1) * T]
+        return carry
+
+    lax.fori_loop(0, CONVS // STEP, project, 0)
 
     rows = lax.broadcasted_iota(jnp.int32, (T, T), 0)
     cols = lax.broadcasted_iota(jnp.int32, (T, T), 1)
@@ -200,9 +236,6 @@
     pos = lax.broadcasted_iota(jnp.int32, (T, 1), 0)
 
     def prepare(g, carry):
-        x = hidden[pl.ds(g * PAIR, PAIR)].reshape(PAIR * T, hidden.shape[-1])
-        projected = mm(x, w_qkvz[...]).astype(BF16)
-        gates = mm(x, wbp[...], 1, 1).astype(BF16).astype(F32)
         rate = jnp.exp(
             jnp.where(lane == 2, decay_log[0], jnp.where(lane == 3, decay_log[1], 0.0))
         )
@@ -211,13 +244,13 @@
         strictly = rows > cols
         tri = jnp.where(inclusive, 1.0, 0.0)
         chains = []
-        for p in range(PAIR):
-            j = g * PAIR + p
+        for p in range(PREP):
+            j = g * PREP + p
             length = lengths[me * CONVS + j]
             owner = owners[me * CONVS + j]
             live = pos < length
-            mixed = projected[p * T : (p + 1) * T, :CH].astype(F32)
-            z_part = projected[p * T : (p + 1) * T, CH:].astype(F32)
+            mixed = proj[j, :, :CH].astype(F32)
+            z_part = proj[j, :, CH:].astype(F32)
             held = cv_recv[owner].astype(F32)
             for i in range(3):
                 for b in range(4):
@@ -229,8 +262,8 @@
             for i in range(3):
                 row = ext[p, pl.ds(5 + length + i, 1), :]
                 for b in range(4):
-                    tail_tmp[i * 4 + b : i * 4 + b + 1, :] = row[:, b * 128 : (b + 1) * 128]
-            fin[j, 2 * DK : 2 * DK + 16, :] = tail_tmp[...].astype(BF16)
+                    tail_tmp[p, i * 4 + b : i * 4 + b + 1, :] = row[:, b * 128 : (b + 1) * 128]
+            fin[j, 2 * DK : 2 * DK + 16, :] = tail_tmp[p].astype(BF16)
             act = silu(convolved)
             q = act[:, :DK]
             k = act[:, DK : 2 * DK]
@@ -241,7 +274,7 @@
                 silu(z_part) * jnp.concatenate([norm_gain[...], norm_gain[...]], axis=1),
                 0.0,
             )
-            raw = gates[p * T : (p + 1) * T, :]
+            raw = gate[j]
             beta = jnp.where(live, 0.5 * jnp.tanh(0.5 * raw) + 0.5, 0.0)
             shifted = raw + bias
             decay = jnp.where(
@@ -275,17 +308,19 @@
         ]
         span = 2
         while span < T:
-            block = (rows // (2 * span) == cols // (2 * span)) & (rows // span != cols // span)
-            left = [mm(jnp.where(block, low, 0.0), inv) for (_, low, _), inv in zip(chains, inverse)]
-            inverse = [inv - mm(inv, part) for inv, part in zip(inverse, left)]
-            span *= 2
+            block = (rows // (4 * span) == cols // (4 * span)) & (rows // span != cols // span)
+            nil = [mm(inv, jnp.where(block, low, 0.0)) for (_, low, _), inv in zip(chains, inverse)]
+            square = [mm(n, n) for n in nil]
+            first = [inv - mm(n, inv) for n, inv in zip(nil, inverse)]
+            inverse = [f + mm(q, f) for q, f in zip(square, first)]
+            span *= 4
         for (at, _, right), inv in zip(chains, inverse):
             solved = mm(inv, right)
             wq[at, :T, :] = solved[:, :DK].astype(BF16)
             u0[at] = solved[:, DK:]
         return carry
 
-    lax.fori_loop(0, CONVS // PAIR, prepare, 0)
+    lax.fori_loop(0, CONVS // PREP, prepare, 0)
 
     def wait_state(d, carry):
         st_copy(d).wait()
@@ -313,7 +348,7 @@
         return carry
 
     def rt_copy(d):
-        peer = lax.rem(me + d, NC)
+        peer = ahead(d)
         return pltpu.make_async_remote_copy(
             src_ref=rt_send.at[peer],
             dst_ref=rt_recv.at[me],
@@ -330,17 +365,18 @@
         return fin[pick]
 
     def send_return(d, carry):
-        peer = lax.rem(me + d, NC)
+        peer = ahead(d)
         rt_send[peer] = return_lane(peer)
         rt_copy(d).start()
         return carry
 
-    def core_copy(j):
+    def norm_copy(g):
+        pair = pl.ds(g * PAIR, PAIR)
         return pltpu.make_async_remote_copy(
-            src_ref=ybuf.at[j, 1 - c],
-            dst_ref=cbuf.at[j],
-            send_sem=co_ss.at[j],
-            recv_sem=co_rs.at[j],
+            src_ref=nrm.at[pair],
+            dst_ref=nrm_other.at[pair],
+            send_sem=nx_ss.at[g],
+            recv_sem=nx_rs.at[g],
             device_id=other,
             device_id_type=MESH,
         )
@@ -360,14 +396,10 @@
             device_id_type=MESH,
         )
 
-    def own_sum(j, dest):
-        return ybuf[j, c, dest].astype(F32) + cbuf[j, dest].astype(F32)
-
     half = T // 2
 
     def far_hop(j):
-        core_copy(j).wait()
-        far = own_sum(j, lax.rem(z + 4, NZ)).astype(BF16)
+        far = ybuf[j, 0].astype(BF16)
         rsend[j, 0, 0, :half, :] = far[:half]
         rsend[j, 1, 0, half:, :] = far[half:]
         ring_copy(j, 0, 0).start()
@@ -376,9 +408,7 @@
     def next_hop(j, hop):
         for way in (0, 1):
             ring_copy(j, way, hop - 1).wait()
-            step = 4 - hop
-            dest = lax.rem(z + (step if way == 0 else NZ - step), NZ)
-            mine = own_sum(j, dest)
+            mine = ybuf[j, NZ - hop if way == 0 else hop]
             if hop == 1:
                 keep = slice(0, half) if way == 0 else slice(half, T)
                 alone = slice(half, T) if way == 0 else slice(0, half)
@@ -390,42 +420,45 @@
                 rsend[j, way, hop] = (mine + came).astype(BF16)
             ring_copy(j, way, hop).start()
 
-    def turn(i, carry):
-        @pl.when(i < CONVS // PAIR)
-        def _():
-            finish(i, 0)
-
-        @pl.when(i < CONVS)
-        def _():
-            normed = nrm[i]
-            for n in range(NZ):
-                y = mm(normed, w_out[:, n * 256 : (n + 1) * 256]).astype(BF16)
-                ybuf[i, 0, n] = y[:, :128]
-                ybuf[i, 1, n] = y[:, 128:]
-            core_copy(i).start()
-
-        @pl.when(i >= 1)
-        def _():
-            far_hop(i - 1)
-
-        @pl.when(i >= 3)
-        def _():
-            next_hop(i - 3, 1)
-
-        return carry
-
-    loads[3].wait()
-    lax.fori_loop(0, CONVS // PAIR, turn, 0)
-    lax.fori_loop(1, NC, send_return, 0)
+    def begin(g):
+        finish(g, 0)
+        norm_copy(g).start()
+
+    def out(g):
+        norm_copy(g).wait()
+        pair = pl.ds(g * PAIR, PAIR)
+        x = jnp.concatenate([nrm[pair].reshape(PAIR * T, 256), nrm_other[pair].reshape(PAIR * T, 256)], axis=1)
+        for n in range(NZ // 2):
+            y = mm(x, w_pair[:, n * 256 : (n + 1) * 256])
+            for p in range(PAIR):
+                for k in range(2):
+                    ybuf[g * PAIR + p, 2 * n + k] = y[p * T : (p + 1) * T, k * 128 : (k + 1) * 128]
+            if n == 0:
+                for p in range(PAIR):
+                    far_hop(g * PAIR + p)
+
+    def hops(g, hop):
+        for p in range(PAIR):
+            next_hop(g * PAIR + p, hop)
+
+    begin(0)
+    begin(1)
+    for r in range(NZ):
+        weight_copy(r).wait()
+    out(0)
+    begin(2)
+    out(1)
+    hops(0, 1)
+    begin(3)
+    for d in ORDER:
+        send_return(d, 0)
     rt_recv[me] = return_lane(me)
-    lax.fori_loop(CONVS // PAIR, CONVS + 1, turn, 0)
-    for hop, first in ((1, CONVS - 2), (2, 0), (3, 0)):
-
-        def hops(j, carry, hop=hop):
-            next_hop(j, hop)
-            return carry
-
-        lax.fori_loop(first, CONVS, hops, 0)
+    out(2)
+    hops(1, 1)
+    hops(0, 2)
+    out(3)
+    for g, hop in ((2, 1), (1, 2), (3, 1), (0, 3), (2, 2), (1, 3), (3, 2), (2, 3), (3, 3)):
+        hops(g, hop)
 
     def wait_return(d, carry):
         rt_copy(d).wait()
@@ -460,7 +493,7 @@
     def last(j, carry):
         ring_copy(j, 0, 3).wait()
         ring_copy(j, 1, 3).wait()
-        total = own_sum(j, z) + rrecv[j, 0, 3].astype(F32) + rrecv[j, 1, 3].astype(F32)
+        total = ybuf[j, 4] + rrecv[j, 0, 3].astype(F32) + rrecv[j, 1, 3].astype(F32)
         layer_out[j] = total.astype(BF16)
         return carry
 
@@ -529,14 +562,16 @@
             dma((SLOTS,)),
             pltpu.VMEM((SLOTS, 16, 128), F32),
             pltpu.VMEM((128, 2048), F32),
+            pltpu.VMEM((CONVS, T, 768), BF16),
+            pltpu.VMEM((CONVS, T, 128), F32),
             pltpu.SMEM((NC,), jnp.int32),
             pltpu.SMEM((NC,), jnp.int32),
             pltpu.VMEM((NC, 16, 128), BF16),
             pltpu.VMEM((NC, 16, 128), BF16),
             pltpu.VMEM((NC, 2 * DK, 128), BF16),
             pltpu.VMEM((NC, 2 * DK, 128), BF16),
-            pltpu.VMEM((PAIR, 8 + T, CH), F32),
-            pltpu.VMEM((16, 128), F32),
+            pltpu.VMEM((PREP, 8 + T, CH), F32),
+            pltpu.VMEM((PREP, 16, 128), F32),
             pltpu.VMEM((2 * CONVS, 2 * T, DK), BF16),
             pltpu.VMEM((2 * CONVS, 2 * T, DK), BF16),
             pltpu.VMEM((2 * CONVS, T, DK), F32),
@@ -546,8 +581,9 @@
             pltpu.VMEM((CONVS, T, 2 * DK), BF16),
             pltpu.VMEM((NC, 2 * DK + 16, 128), BF16),
             pltpu.VMEM((NC, 2 * DK + 16, 128), BF16),
-            pltpu.VMEM((CONVS, 2, NZ, T, 128), BF16),
-            pltpu.VMEM((CONVS, NZ, T, 128), BF16),
+            pltpu.VMEM((CONVS, T, 2 * DK), BF16),
+            pltpu.VMEM((512, 1024), BF16),
+            pltpu.VMEM((CONVS, NZ, T, 128), F32),
             pltpu.VMEM((CONVS, 2, 4, T, 128), BF16),
             pltpu.VMEM((CONVS, 2, 4, T, 128), BF16),
             pltpu.VMEM((3, SLOTS, CH), F32),
@@ -557,8 +593,10 @@
             dma((NC,)),
             dma((NC,)),
             dma((NC,)),
-            dma((CONVS,)),
-            dma((CONVS,)),
+            dma((CONVS // PAIR,)),
+            dma((CONVS // PAIR,)),
+            dma((NZ,)),
+            dma((NZ,)),
             dma((CONVS, 2, 4)),
             dma((CONVS, 2, 4)),
         ],

time: 65.2 us -> 60.6 us (0.929); the launches traced: 64.1 us -> 60.3 us
  Pallas kernels: 63.4 us -> 59.7 us
    pallas_call x1, Pallas kernels: 60.9 us -> 57.2 us  [local(): pl.pallas_call(kernel, out_shape=results, in_specs=[far, smem, smem, smem...]
where the time goes in v3:
time: 60.6 us; the launch traced here: 60.3 us
  Pallas kernels  59.7 us (99%)
  between operations  0.64 us (1%)
    pallas_call x1, Pallas kernels, local(): pl.pallas_call(kernel, out_shape=results, in_specs=[far, smem, smem, smem...  57.2 us
    pallas_call x1, Pallas kernels, local(): pl.pallas_call(hand_on, out_shape=results, in_specs=[hbm, hbm, hbm], out_...  2.54 us

profile of v3, /device:TPU:2, one launch (start us, length us, event | category | flops | bytes accessed | tf_op | source)
XLA Modules:
  0.0 60.3 jit_solution(15796956692038017806)
XLA Ops:
  0.6 57.2 %shard_map.148 = (bf16[8,128,128]{2,1,0:T(8,128)(2,1)}, f32[16,256,128]{2,1,0:T(8,128)}, bf16[3,16,512]{2,1,0:T(8,128)(2,1)}) custom-call(bf16[8,128,2048]{2,1,0:T(8,128)(2,1)} %hidden_in.1, s32[128]{0:T(128)} %lengths.1, s32[128]{0:T(128)} %owners.1, s32[128]{0:T(128)} %slots.1, f32[16,256,128]{2,1,0:T(8,128)} %bitcast.19, bf16[3,16,512]{2,1,0:T(8,128)(2,1)} %bitcast.20, ...), custom_call_target="tpu_custom_call" | custom-call | tf_op jit(solution)/shard_map/pallas_call | solution.py:550
  57.8 2.5 %shard_map.149 = (bf16[8,128,128]{2,1,0:T(8,128)(2,1)}, f32[16,256,128]{2,1,0:T(8,128)}, bf16[3,16,512]{2,1,0:T(8,128)(2,1)}) custom-call(bf16[8,128,128]{2,1,0:T(8,128)(2,1)} %get-tuple-element.9.layer_in, f32[16,256,128]{2,1,0:T(8,128)} %get-tuple-element.10.state_in, bf16[3,16,512]{2,1,0:T(8,128)(2,1)} %get-tuple-element.11.conv_in), custom_call_target="tpu_custom_call" | custom-call | tf_op jit(solution)/shard_map/pallas_call | solution.py:621

commit v4 on v3

--- a/solution.py
+++ b/solution.py
@@ -18,6 +18,7 @@
 DK = 128
 CH = 512
 SLOTS = 16
+EARLY = 2
 PAIR = 2
 STEP = 2
 PREP = 4
@@ -56,6 +57,7 @@
     w_qkvz,
     w_out,
     new_state,
+    layer,
     in_s,
     out_s,
     convl,
@@ -82,6 +84,8 @@
     nrm_other,
     w_pair,
     ybuf,
+    rsend0,
+    rrecv0,
     rsend,
     rrecv,
     newcf,
@@ -133,15 +137,14 @@
         for i in range(3):
             for b in range(4):
                 convl[s, i * 4 + b : i * 4 + b + 1, :] = newcf[i, s : s + 1, b * 128 : (b + 1) * 128]
-    pl.semaphore_wait(barrier, NC - 1 + 3)
 
     def cv_copy(d):
         peer = ahead(d)
         return pltpu.make_async_remote_copy(
             src_ref=cv_send.at[peer],
             dst_ref=cv_recv.at[me],
-            send_sem=cv_ss.at[d],
-            recv_sem=cv_rs.at[d],
+            send_sem=cv_ss,
+            recv_sem=cv_rs,
             device_id=(peer, tt),
             device_id_type=MESH,
         )
@@ -151,11 +154,22 @@
         return pltpu.make_async_remote_copy(
             src_ref=st_send.at[peer],
             dst_ref=st_recv.at[me],
-            send_sem=st_ss.at[d],
-            recv_sem=st_rs.at[d],
+            send_sem=st_ss,
+            recv_sem=st_rs,
             device_id=(peer, tt),
             device_id_type=MESH,
         )
+
+    def settle(sent, came, send_sem, recv_sem):
+        lanes = pl.ds(0, NC - 1)
+        pltpu.make_async_remote_copy(
+            src_ref=sent.at[lanes],
+            dst_ref=came.at[lanes],
+            send_sem=send_sem,
+            recv_sem=recv_sem,
+            device_id=(ahead(1), tt),
+            device_id_type=MESH,
+        ).wait()
 
     def conv_lane(peer):
         slot = jnp.int32(0)
@@ -170,20 +184,27 @@
 
     tail_tmp[...] = jnp.zeros_like(tail_tmp)
 
+    def pack_conv(peer, carry):
+        cv_send[peer] = conv_lane(peer)
+        return carry
+
+    lax.fori_loop(0, NC, pack_conv, 0)
+    cv_recv[me] = cv_send[me]
+    pl.semaphore_wait(barrier, NC - 1 + 3)
+
     def send_conv(d, carry):
-        peer = ahead(d)
-        cv_send[peer] = conv_lane(peer)
         cv_copy(d).start()
         return carry
 
     lax.fori_loop(1, NC, send_conv, 0)
-    cv_recv[me] = conv_lane(me)
 
     loads[0].wait()
 
-    for d in ORDER:
+    for n, d in enumerate(ORDER):
         peer = ahead(d)
         st_send[peer] = state[serve_slot[peer]].astype(BF16)
+        if n < EARLY:
+            st_copy(d).start()
     st_recv[me] = state[serve_slot[me]].astype(BF16)
 
     def columns(r, core):
@@ -193,8 +214,8 @@
         return pltpu.make_async_remote_copy(
             src_ref=w_out.at[:, columns(r, 1 - c)],
             dst_ref=w_pair.at[pl.ds(256, 256), pl.ds(r * 128, 128)],
-            send_sem=co_ss.at[r],
-            recv_sem=co_rs.at[r],
+            send_sem=co_ss,
+            recv_sem=co_rs,
             device_id=other,
             device_id_type=MESH,
         )
@@ -205,13 +226,9 @@
     for r in range(NZ):
         w_pair[0:256, r * 128 : (r + 1) * 128] = w_out[:, columns(r, c)]
 
-    def wait_conv(d, carry):
-        cv_copy(d).wait()
-        return carry
-
-    lax.fori_loop(1, NC, wait_conv, 0)
-
-    for d in ORDER:
+    settle(cv_send, cv_recv, cv_ss, cv_rs)
+
+    for d in ORDER[EARLY:]:
         st_copy(d).start()
 
     wbp[...] = jnp.zeros_like(wbp)
@@ -322,11 +339,7 @@
 
     lax.fori_loop(0, CONVS // PREP, prepare, 0)
 
-    def wait_state(d, carry):
-        st_copy(d).wait()
-        return carry
-
-    lax.fori_loop(1, NC, wait_state, 0)
+    settle(st_send, st_recv, st_ss, st_rs)
 
     def finish(g, carry):
         for p in range(PAIR):
@@ -352,8 +365,8 @@
         return pltpu.make_async_remote_copy(
             src_ref=rt_send.at[peer],
             dst_ref=rt_recv.at[me],
-            send_sem=rt_ss.at[d],
-            recv_sem=rt_rs.at[d],
+            send_sem=rt_ss,
+            recv_sem=rt_rs,
             device_id=(peer, tt),
             device_id_type=MESH,
         )
@@ -375,57 +388,53 @@
         return pltpu.make_async_remote_copy(
             src_ref=nrm.at[pair],
             dst_ref=nrm_other.at[pair],
-            send_sem=nx_ss.at[g],
+            send_sem=nx_ss,
             recv_sem=nx_rs.at[g],
             device_id=other,
             device_id_type=MESH,
         )
 
-    def ring_copy(j, way, hop):
-        if hop == 0:
-            part = pl.ds(way * (T // 2), T // 2)
-            src, dst = rsend.at[j, way, hop, part], rrecv.at[j, way, hop, part]
-        else:
-            src, dst = rsend.at[j, way, hop], rrecv.at[j, way, hop]
+    def ring_copy(src, dst, way, g, hop):
         return pltpu.make_async_remote_copy(
             src_ref=src,
             dst_ref=dst,
-            send_sem=ri_ss.at[j, way, hop],
-            recv_sem=ri_rs.at[j, way, hop],
+            send_sem=ri_ss.at[min(hop, 1)],
+            recv_sem=ri_rs.at[g, hop],
             device_id=up if way == 0 else down,
             device_id_type=MESH,
         )
 
     half = T // 2
 
-    def far_hop(j):
+    def far_hop(j, g):
         far = ybuf[j, 0].astype(BF16)
-        rsend[j, 0, 0, :half, :] = far[:half]
-        rsend[j, 1, 0, half:, :] = far[half:]
-        ring_copy(j, 0, 0).start()
-        ring_copy(j, 1, 0).start()
-
-    def next_hop(j, hop):
         for way in (0, 1):
-            ring_copy(j, way, hop - 1).wait()
+            rsend0[j, way] = far[way * half : (way + 1) * half]
+            ring_copy(rsend0.at[j, way], rrecv0.at[j, way], way, g, 0).start()
+
+    def came(g, hop):
+        pair = pl.ds(g * PAIR, PAIR)
+        ref = rrecv0.at[pair] if hop == 0 else rrecv.at[hop - 1, pair]
+        ring_copy(ref, ref, 0, g, hop).wait_recv()
+
+    def next_hop(j, g, hop):
+        for way in (0, 1):
             mine = ybuf[j, NZ - hop if way == 0 else hop]
             if hop == 1:
-                keep = slice(0, half) if way == 0 else slice(half, T)
-                alone = slice(half, T) if way == 0 else slice(0, half)
-                came = rrecv[j, way, 0, keep, :].astype(F32)
-                rsend[j, way, hop, keep, :] = (mine[keep] + came).astype(BF16)
-                rsend[j, way, hop, alone, :] = mine[alone].astype(BF16)
+                keep = slice(way * half, (way + 1) * half)
+                alone = slice((1 - way) * half, (2 - way) * half)
+                rsend[0, j, way, keep, :] = (mine[keep] + rrecv0[j, way].astype(F32)).astype(BF16)
+                rsend[0, j, way, alone, :] = mine[alone].astype(BF16)
             else:
-                came = rrecv[j, way, hop - 1].astype(F32)
-                rsend[j, way, hop] = (mine + came).astype(BF16)
-            ring_copy(j, way, hop).start()
+                rsend[hop - 1, j, way] = (mine + rrecv[hop - 2, j, way].astype(F32)).astype(BF16)
+            ring_copy(rsend.at[hop - 1, j, way], rrecv.at[hop - 1, j, way], way, g, hop).start()
 
     def begin(g):
         finish(g, 0)
         norm_copy(g).start()
 
     def out(g):
-        norm_copy(g).wait()
+        norm_copy(g).wait_recv()
         pair = pl.ds(g * PAIR, PAIR)
         x = jnp.concatenate([nrm[pair].reshape(PAIR * T, 256), nrm_other[pair].reshape(PAIR * T, 256)], axis=1)
         for n in range(NZ // 2):
@@ -435,16 +444,24 @@
                     ybuf[g * PAIR + p, 2 * n + k] = y[p * T : (p + 1) * T, k * 128 : (k + 1) * 128]
             if n == 0:
                 for p in range(PAIR):
-                    far_hop(g * PAIR + p)
+                    far_hop(g * PAIR + p, g)
 
     def hops(g, hop):
+        came(g, hop - 1)
         for p in range(PAIR):
-            next_hop(g * PAIR + p, hop)
+            next_hop(g * PAIR + p, g, hop)
 
     begin(0)
     begin(1)
-    for r in range(NZ):
-        weight_copy(r).wait()
+    rows_other = w_pair.at[pl.ds(256, 256)]
+    pltpu.make_async_remote_copy(
+        src_ref=rows_other,
+        dst_ref=rows_other,
+        send_sem=co_ss,
+        recv_sem=co_rs,
+        device_id=other,
+        device_id_type=MESH,
+    ).wait()
     out(0)
     begin(2)
     out(1)
@@ -460,14 +477,10 @@
     for g, hop in ((2, 1), (1, 2), (3, 1), (0, 3), (2, 2), (1, 3), (3, 2), (2, 3), (3, 3)):
         hops(g, hop)
 
-    def wait_return(d, carry):
-        rt_copy(d).wait()
-        return carry
-
-    lax.fori_loop(1, NC, wait_return, 0)
+    settle(rt_send, rt_recv, rt_ss, rt_rs)
 
     def leave(s):
-        return pltpu.make_async_copy(new_state.at[s], new_state_out.at[s], out_s.at[s])
+        return pltpu.make_async_copy(new_state.at[s], new_state_out.at[s], out_s.at[0])
 
     def store(s, carry):
         source = jnp.int32(0)
@@ -490,20 +503,27 @@
                 newcf[i, s : s + 1, b * 128 : (b + 1) * 128] = convl[s, i * 4 + b : i * 4 + b + 1, :]
     new_conv[...] = newcf[...].astype(BF16)
 
-    def last(j, carry):
-        ring_copy(j, 0, 3).wait()
-        ring_copy(j, 1, 3).wait()
-        total = ybuf[j, 4] + rrecv[j, 0, 3].astype(F32) + rrecv[j, 1, 3].astype(F32)
-        layer_out[j] = total.astype(BF16)
-        return carry
-
-    lax.fori_loop(0, CONVS, last, 0)
-
-    def left(s, carry):
-        leave(s).wait()
-        return carry
-
-    lax.fori_loop(0, SLOTS, left, 0)
+    for g in range(CONVS // PAIR):
+        came(g, 3)
+        for p in range(PAIR):
+            j = g * PAIR + p
+            total = ybuf[j, 4] + rrecv[2, j, 0].astype(F32) + rrecv[2, j, 1].astype(F32)
+            layer[j] = total.astype(BF16)
+        pair = pl.ds(g * PAIR, PAIR)
+        pltpu.make_async_copy(layer.at[pair], layer_out.at[pair], out_s.at[1]).start()
+
+    ring_copy(rsend0, rrecv0, 0, 0, 0).wait_send()
+    ring_copy(rsend, rrecv, 0, 0, 1).wait_send()
+    pltpu.make_async_remote_copy(
+        src_ref=nrm,
+        dst_ref=nrm_other,
+        send_sem=nx_ss,
+        recv_sem=nx_rs.at[0],
+        device_id=other,
+        device_id_type=MESH,
+    ).wait_send()
+    pltpu.make_async_copy(new_state, new_state_out, out_s.at[0]).wait()
+    pltpu.make_async_copy(layer, layer_out, out_s.at[1]).wait()
 
 
 def hand_on(layer_in, state_in, conv_in, layer_out, state_out, conv_out, layer, state, conv, came, gone):
@@ -551,15 +571,16 @@
         kernel,
         out_shape=results,
         in_specs=[far, smem, smem, smem, far, vmem, far, vmem, vmem, smem, smem, vmem, far],
-        out_specs=(vmem, far, vmem),
+        out_specs=(far, far, vmem),
         scratch_shapes=[
             pltpu.VMEM((CONVS, T, 2048), BF16),
             pltpu.VMEM((SLOTS, 2 * DK, 128), F32),
             pltpu.VMEM((2048, 768), BF16),
             pltpu.VMEM((256, 2048), BF16),
             pltpu.VMEM((SLOTS, 2 * DK, 128), F32),
+            pltpu.VMEM((CONVS, T, 128), BF16),
             dma((4,)),
-            dma((SLOTS,)),
+            dma((2,)),
             pltpu.VMEM((SLOTS, 16, 128), F32),
             pltpu.VMEM((128, 2048), F32),
             pltpu.VMEM((CONVS, T, 768), BF16),
@@ -584,21 +605,23 @@
             pltpu.VMEM((CONVS, T, 2 * DK), BF16),
             pltpu.VMEM((512, 1024), BF16),
             pltpu.VMEM((CONVS, NZ, T, 128), F32),
-            pltpu.VMEM((CONVS, 2, 4, T, 128), BF16),
-            pltpu.VMEM((CONVS, 2, 4, T, 128), BF16),
+            pltpu.VMEM((CONVS, 2, T // 2, 128), BF16),
+            pltpu.VMEM((CONVS, 2, T // 2, 128), BF16),
+            pltpu.VMEM((3, CONVS, 2, T, 128), BF16),
+            pltpu.VMEM((3, CONVS, 2, T, 128), BF16),
             pltpu.VMEM((3, SLOTS, CH), F32),
-            dma((NC,)),
-            dma((NC,)),
-            dma((NC,)),
-            dma((NC,)),
-            dma((NC,)),
-            dma((NC,)),
+            dma(()),
+            dma(()),
+            dma(()),
+            dma(()),
+            dma(()),
+            dma(()),
+            dma(()),
             dma((CONVS // PAIR,)),
-            dma((CONVS // PAIR,)),
-            dma((NZ,)),
-            dma((NZ,)),
-            dma((CONVS, 2, 4)),
-            dma((CONVS, 2, 4)),
+            dma(()),
+            dma(()),
+            dma((2,)),
+            dma((CONVS // PAIR, 4)),
         ],
         compiler_params=pltpu.CompilerParams(
             collective_id=0, has_side_effects=True, vmem_limit_bytes=56 * 1024 * 1024

time: 60.6 us -> 59.5 us (0.982)
  Pallas kernels: 59.7 us -> 58.5 us
    pallas_call x1, Pallas kernels: 57.2 us -> 56 us  [local(): pl.pallas_call(kernel, out_shape=results, in_specs=[far, smem, smem, smem...]
where the time goes in v4:
time: 59.5 us; the launch traced here: 59.2 us
  Pallas kernels  58.5 us (98%)
  between operations  0.64 us (1%)
    pallas_call x1, Pallas kernels, local(): pl.pallas_call(kernel, out_shape=results, in_specs=[far, smem, smem, smem...  56 us
    pallas_call x1, Pallas kernels, local(): pl.pallas_call(hand_on, out_shape=results, in_specs=[hbm, hbm, hbm], out_...  2.54 us

profile of v4, /device:TPU:2, one launch (start us, length us, event | category | flops | bytes accessed | tf_op | source)
XLA Modules:
  0.0 59.2 jit_solution(9295754723359121813)
XLA Ops:
  0.6 56.0 %shard_map.148 = (bf16[8,128,128]{2,1,0:T(8,128)(2,1)}, f32[16,256,128]{2,1,0:T(8,128)}, bf16[3,16,512]{2,1,0:T(8,128)(2,1)}) custom-call(bf16[8,128,2048]{2,1,0:T(8,128)(2,1)} %hidden_in.1, s32[128]{0:T(128)} %lengths.1, s32[128]{0:T(128)} %owners.1, s32[128]{0:T(128)} %slots.1, f32[16,256,128]{2,1,0:T(8,128)} %bitcast.19, bf16[3,16,512]{2,1,0:T(8,128)(2,1)} %bitcast.20, ...), custom_call_target="tpu_custom_call" | custom-call | tf_op jit(solution)/shard_map/pallas_call | solution.py:570
  56.6 2.5 %shard_map.149 = (bf16[8,128,128]{2,1,0:T(8,128)(2,1)}, f32[16,256,128]{2,1,0:T(8,128)}, bf16[3,16,512]{2,1,0:T(8,128)(2,1)}) custom-call(bf16[8,128,128]{2,1,0:T(8,128)(2,1)} %get-tuple-element.9.layer_in, f32[16,256,128]{2,1,0:T(8,128)} %get-tuple-element.10.state_in, bf16[3,16,512]{2,1,0:T(8,128)(2,1)} %get-tuple-element.11.conv_in), custom_call_target="tpu_custom_call" | custom-call | tf_op jit(solution)/shard_map/pallas_call | solution.py:644

commit v5 on v4

--- a/solution.py
+++ b/solution.py
@@ -20,8 +20,8 @@
 SLOTS = 16
 EARLY = 2
 PAIR = 2
-STEP = 2
-PREP = 4
+STEP = 4
+PREP = 8
 ORDER = sorted(range(1, NC), key=lambda n: -(min(n // 4, 4 - n // 4) + min(n % 4, 4 - n % 4)))
 
 
@@ -128,7 +128,8 @@
         pl.semaphore_signal(barrier, inc=1, device_id=(ahead(d), tt), device_id_type=MESH)
         return carry
 
-    lax.fori_loop(1, NC, greet, 0)
+    for d in ORDER:
+        greet(d, 0)
     for peer in (other, up, down):
         pl.semaphore_signal(barrier, inc=1, device_id=peer, device_id_type=MESH)
     newcf[...] = conv_cache[...].astype(F32)
@@ -196,7 +197,8 @@
         cv_copy(d).start()
         return carry
 
-    lax.fori_loop(1, NC, send_conv, 0)
+    for d in ORDER:
+        send_conv(d, 0)
 
     loads[0].wait()
 
@@ -474,7 +476,7 @@
     hops(1, 1)
     hops(0, 2)
     out(3)
-    for g, hop in ((2, 1), (1, 2), (3, 1), (0, 3), (2, 2), (1, 3), (3, 2), (2, 3), (3, 3)):
+    for g, hop in ((2, 1), (3, 1), (1, 2), (2, 2), (3, 2), (0, 3), (1, 3), (2, 3), (3, 3)):
         hops(g, hop)
 
     settle(rt_send, rt_recv, rt_ss, rt_rs)

time: 59.5 us -> 56.5 us (0.950)
  Pallas kernels: 58.5 us -> 55.7 us
    pallas_call x1, Pallas kernels: 56 us -> 53.1 us  [local(): pl.pallas_call(kernel, out_shape=results, in_specs=[far, smem, smem, smem...]
where the time goes in v5:
time: 56.5 us; the launch traced here: 56.3 us
  Pallas kernels  55.7 us (99%)
  between operations  0.64 us (1%)
    pallas_call x1, Pallas kernels, local(): pl.pallas_call(kernel, out_shape=results, in_specs=[far, smem, smem, smem...  53.1 us
    pallas_call x1, Pallas kernels, local(): pl.pallas_call(hand_on, out_shape=results, in_specs=[hbm, hbm, hbm], out_...  2.54 us

profile of v5, /device:TPU:2, one launch (start us, length us, event | category | flops | bytes accessed | tf_op | source)
XLA Modules:
  0.0 56.3 jit_solution(7974561479472617485)
XLA Ops:
  0.6 53.1 %shard_map.148 = (bf16[8,128,128]{2,1,0:T(8,128)(2,1)}, f32[16,256,128]{2,1,0:T(8,128)}, bf16[3,16,512]{2,1,0:T(8,128)(2,1)}) custom-call(bf16[8,128,2048]{2,1,0:T(8,128)(2,1)} %hidden_in.1, s32[128]{0:T(128)} %lengths.1, s32[128]{0:T(128)} %owners.1, s32[128]{0:T(128)} %slots.1, f32[16,256,128]{2,1,0:T(8,128)} %bitcast.19, bf16[3,16,512]{2,1,0:T(8,128)(2,1)} %bitcast.20, ...), custom_call_target="tpu_custom_call" | custom-call | tf_op jit(solution)/shard_map/pallas_call | solution.py:572
  53.8 2.5 %shard_map.149 = (bf16[8,128,128]{2,1,0:T(8,128)(2,1)}, f32[16,256,128]{2,1,0:T(8,128)}, bf16[3,16,512]{2,1,0:T(8,128)(2,1)}) custom-call(bf16[8,128,128]{2,1,0:T(8,128)(2,1)} %get-tuple-element.9.layer_in, f32[16,256,128]{2,1,0:T(8,128)} %get-tuple-element.10.state_in, bf16[3,16,512]{2,1,0:T(8,128)(2,1)} %get-tuple-element.11.conv_in), custom_call_target="tpu_custom_call" | custom-call | tf_op jit(solution)/shard_map/pallas_call | solution.py:646

commit v6 on v5

--- a/solution.py
+++ b/solution.py
@@ -18,7 +18,7 @@
 DK = 128
 CH = 512
 SLOTS = 16
-EARLY = 2
+EARLY = 8
 PAIR = 2
 STEP = 4
 PREP = 8
@@ -206,7 +206,10 @@
         peer = ahead(d)
         st_send[peer] = state[serve_slot[peer]].astype(BF16)
         if n < EARLY:
-            st_copy(d).start()
+
+            @pl.when(c == 0)
+            def _(d=d):
+                st_copy(d).start()
     st_recv[me] = state[serve_slot[me]].astype(BF16)
 
     def columns(r, core):
@@ -222,16 +225,22 @@
             device_id_type=MESH,
         )
 
+    settle(cv_send, cv_recv, cv_ss, cv_rs)
+
+    for n, d in enumerate(ORDER):
+        if n < EARLY:
+
+            @pl.when(c == 1)
+            def _(d=d):
+                st_copy(d).start()
+        else:
+            st_copy(d).start()
+
     loads[1].wait()
     for r in range(NZ):
         weight_copy(r).start()
     for r in range(NZ):
         w_pair[0:256, r * 128 : (r + 1) * 128] = w_out[:, columns(r, c)]
-
-    settle(cv_send, cv_recv, cv_ss, cv_rs)
-
-    for d in ORDER[EARLY:]:
-        st_copy(d).start()
 
     wbp[...] = jnp.zeros_like(wbp)
     wbp[0:4, :] = w_ba[...].astype(F32)

time: 56.5 us -> 56.3 us (level)
  no operation moved by 1% of the time
where the time goes in v6:
time: 56.3 us; the launch traced here: 56 us
  Pallas kernels  55.4 us (98%)
  between operations  0.64 us (1%)
    pallas_call x1, Pallas kernels, local(): pl.pallas_call(kernel, out_shape=results, in_specs=[far, smem, smem, smem...  52.8 us
    pallas_call x1, Pallas kernels, local(): pl.pallas_call(hand_on, out_shape=results, in_specs=[hbm, hbm, hbm], out_...  2.54 us

profile of v6, /device:TPU:2, one launch (start us, length us, event | category | flops | bytes accessed | tf_op | source)
XLA Modules:
  0.0 56.0 jit_solution(6048862289137121518)
XLA Ops:
  0.6 52.8 %shard_map.148 = (bf16[8,128,128]{2,1,0:T(8,128)(2,1)}, f32[16,256,128]{2,1,0:T(8,128)}, bf16[3,16,512]{2,1,0:T(8,128)(2,1)}) custom-call(bf16[8,128,2048]{2,1,0:T(8,128)(2,1)} %hidden_in.1, s32[128]{0:T(128)} %lengths.1, s32[128]{0:T(128)} %owners.1, s32[128]{0:T(128)} %slots.1, f32[16,256,128]{2,1,0:T(8,128)} %bitcast.19, bf16[3,16,512]{2,1,0:T(8,128)(2,1)} %bitcast.20, ...), custom_call_target="tpu_custom_call" | custom-call | tf_op jit(solution)/shard_map/pallas_call | solution.py:581
  53.5 2.5 %shard_map.149 = (bf16[8,128,128]{2,1,0:T(8,128)(2,1)}, f32[16,256,128]{2,1,0:T(8,128)}, bf16[3,16,512]{2,1,0:T(8,128)(2,1)}) custom-call(bf16[8,128,128]{2,1,0:T(8,128)(2,1)} %get-tuple-element.9.layer_in, f32[16,256,128]{2,1,0:T(8,128)} %get-tuple-element.10.state_in, bf16[3,16,512]{2,1,0:T(8,128)(2,1)} %get-tuple-element.11.conv_in), custom_call_target="tpu_custom_call" | custom-call | tf_op jit(solution)/shard_map/pallas_call | solution.py:655
